TPU v7x, 256 devices: a whole 4x4x8 slice. The times are simulated.
256 devices in a mesh: ctx: 64 (over z, y, core), kv: 4 (over x).
Axes of the slice: x: 4, y: 4, z: 8, core: 2. Of those that a mesh axis runs over, the one named last changes fastest.
Arguments:
- query: bfloat16 [2, 8192, 8192], P(None, 'ctx', 'kv')
- kv_rows: bfloat16 [2, 8192, 2048], P(None, 'ctx', 'kv')
- keep: int32 [2, 64, 8, 512], P(None, 'ctx', 'kv'), may hold values from 0 to 639, as said below
- dest: int32 [65536, 1], P('ctx'), may hold values from 0 to 255; in each aligned block of 1024 rows (0 to 1023, 1024 to 2047, ...) at most 8 rows name the same one
- offsets: int32 [2], replicated, may hold values from 0 to 62, as said below
Outputs:
- attention: bfloat16 [2, 8192, 8192], P(None, 'ctx', 'kv')
- row_scores: float32 [2, 8, 40960], P(None, 'kv', 'ctx')
- owner_cache: bfloat16 [131072, 2048], P(('ctx', 'kv'))
Inputs may be any that keep to these rules, and one draw needn't show every extreme that they name: `keep`: each list holds 512 distinct indices in increasing order; an index below 512 names a cache slot, an index k of 512 or more names span row k - 512. `dest`: among the 1024 rows of one context shard no owner is named more than 8 times; owner o is the device at position o in the ctx-major order of ctx and kv. `offsets`: one prompt starts at the first shard and another prompt at the second-to-last shard.
All inputs are finite; a program needn't handle non-finite values.
Results may differ from a plain program's by a relative error of at most 0.0049.
Values may be sent and summed in bfloat16 or wider, within the bound.
A program may use at most 192 MiB of HBM per device.

v0:
```python
import math

import jax
import jax.numpy as jnp
from jax import lax
from jax.sharding import PartitionSpec as P

HEAD = 128


def carried_in(value, axis, join, neutral):
    count, mine = (lax.axis_size(axis), lax.axis_index(axis))
    pieces = jax.tree.map(lambda part: lax.all_gather(part, axis), value)
    subtotal = jax.tree.map(
        lambda part, zero: jnp.full_like(part, 0) + jnp.asarray(zero, part.dtype), value, neutral
    )

    def hop(position, subtotal):
        longer = join(subtotal, jax.tree.map(lambda part: part[position], pieces))
        return jax.tree.map(lambda new, old: jnp.where(position < mine, new, old), longer, subtotal)

    return lax.fori_loop(0, count - 1, hop, subtotal)


def compose(earlier, later):
    early_marks, early_rows = earlier
    late_marks, late_rows = later
    length = late_marks.shape[-1]
    table = late_marks[..., None] == jnp.arange(length, dtype=jnp.int32)
    picked_marks = jnp.sum(jnp.where(table, early_marks[..., None, :], 0), axis=-1)
    marks = jnp.where(late_marks < length, picked_marks, late_marks)
    moved = jnp.einsum(
        "phst,pthc->pshc",
        table.astype(jnp.bfloat16),
        early_rows,
        preferred_element_type=jnp.float32,
    ).astype(jnp.bfloat16)
    carried = jnp.transpose(late_marks < length, (0, 2, 1))[..., None]
    rows = jnp.where(carried, moved, late_rows)
    return (marks.astype(jnp.int32), rows)


def local(query, kv_rows, keep, dest, offsets):
    prompts, span, qwidth = query.shape
    width = 2 * HEAD
    heads_dev = kv_rows.shape[2] // width
    cache_len = keep.shape[3]
    group = qwidth // (HEAD * heads_dev)
    position = lax.axis_index("ctx")
    active = position >= offsets
    keep_local = keep[:, 0]
    span_kv = kv_rows.reshape(prompts, span, heads_dev, width)
    slots = jnp.broadcast_to(
        jnp.arange(cache_len, dtype=jnp.int32), (prompts, heads_dev, cache_len)
    )
    own_marks = jnp.where(keep_local < cache_len, keep_local, cache_len)
    own_marks = jnp.where(active[:, None, None], own_marks, slots)
    picker = (keep_local[..., None] - cache_len == jnp.arange(span, dtype=jnp.int32)).astype(
        jnp.bfloat16
    )
    own_rows = jnp.einsum(
        "phst,pthc->pshc", picker, span_kv, preferred_element_type=jnp.float32
    ).astype(jnp.bfloat16)
    own_rows = jnp.where(active[:, None, None, None], own_rows, jnp.zeros_like(own_rows))
    identity = (slots, jnp.zeros_like(own_rows))
    incoming = carried_in((own_marks, own_rows), "ctx", compose, identity)
    in_marks, in_rows = incoming
    outgoing = compose(incoming, (own_marks, own_rows))
    rows_all = jnp.concatenate([in_rows, span_kv], axis=1)
    valid = in_marks >= cache_len
    qfive = query.reshape(prompts, span, heads_dev, group, HEAD)
    causal = jnp.arange(span)[None, :] <= jnp.arange(span)[:, None]
    scale = 1.0 / math.sqrt(HEAD)
    outputs = []
    masses = []
    for prompt in range(prompts):
        flag = active[prompt].astype(jnp.float32)
        head_outs = []
        head_mass = []
        for head in range(heads_dev):
            keys = rows_all[prompt, :, head, :HEAD]
            values = rows_all[prompt, :, head, HEAD:]
            attention_scores = (
                jnp.einsum(
                    "qgd,kd->gqk", qfive[prompt, :, head], keys, preferred_element_type=jnp.float32
                )
                * scale
            )
            seen = jnp.broadcast_to(valid[prompt, head][None, :], (span, cache_len))
            allowed = jnp.concatenate([seen, causal], axis=1)[None]
            attention_scores = jnp.where(allowed, attention_scores, -1e30)
            peak = jnp.max(attention_scores, axis=-1, keepdims=True)
            expo = jnp.where(allowed, jnp.exp(attention_scores - peak), 0.0)
            weights = expo / jnp.sum(expo, axis=-1, keepdims=True)
            mixed = jnp.einsum(
                "gqk,kd->qgd",
                weights.astype(jnp.bfloat16),
                values,
                preferred_element_type=jnp.float32,
            )
            head_outs.append((mixed * flag).astype(jnp.bfloat16))
            head_mass.append(jnp.sum(weights, axis=(0, 1)) * flag)
        outputs.append(jnp.stack(head_outs, axis=1))
        masses.append(jnp.stack(head_mass, axis=0))
    attention = jnp.stack(outputs, axis=0).reshape(prompts, span, qwidth)
    row_scores = jnp.stack(masses, axis=0)
    owner_count = lax.axis_size("ctx") * lax.axis_size("kv")
    capacity = 2 * prompts * cache_len // owner_count
    sending = outgoing[1].reshape(prompts * cache_len, heads_dev * width)
    owner_ids = dest[:, 0]
    onehot = (owner_ids[:, None] == jnp.arange(owner_count, dtype=jnp.int32)).astype(jnp.int32)
    rank = jnp.sum((jnp.cumsum(onehot, axis=0) - 1) * onehot, axis=1)
    target = owner_ids * capacity + rank
    placing = (
        target[None, :] == jnp.arange(owner_count * capacity, dtype=jnp.int32)[:, None]
    ).astype(jnp.bfloat16)
    packed = jnp.dot(placing, sending, preferred_element_type=jnp.float32).astype(jnp.bfloat16)
    packed = packed.reshape(lax.axis_size("ctx"), lax.axis_size("kv"), capacity, heads_dev * width)
    arrived = lax.all_to_all(
        lax.all_to_all(packed, "ctx", split_axis=0, concat_axis=0, tiled=True),
        "kv",
        split_axis=1,
        concat_axis=3,
        tiled=True,
    )
    owner_cache = arrived.reshape(-1, arrived.shape[3])
    return (attention, row_scores, owner_cache)


def solution(mesh):
    placed = (
        P(None, "ctx", "kv"),
        P(None, "ctx", "kv"),
        P(None, "ctx", "kv", None),
        P("ctx", None),
        P(),
    )
    return jax.shard_map(
        local,
        mesh=mesh,
        in_specs=placed,
        out_specs=(P(None, "ctx", "kv"), P(None, "kv", "ctx"), P(("ctx", "kv"), None)),
        check_vma=False,
    )
```

profile of v0, /device:TPU:1, one launch (start us, length us, event | category | flops | bytes accessed | tf_op | source)
XLA Modules:
  0.0 564.7 jit_solution(11673814230573235167)
XLA Ops:
  15.5 54.9 %all_gather.10 = s32[64,2,2,512]{3,2,1,0:T(2,128)S(1)} all-gather(s32[1,2,2,512]{3,2,1,0:T(2,128)S(1)} %fusion.131), channel_id=1, replica_groups=mesh['ctx'=64,'kv'=4] {'ctx'}, dimensions={0}, use_global_device_ids=true | all-gather | bytes 532480 | tf_op jit(solution)/shard_map/all_gather | solution.py:13
  70.9 182.5 %all-gather.3.cloned.1.call-done = bf16[128,512,2,256]{3,1,2,0:T(8,128)(2,1)} async-done(((bf16[2,512,2,256]{3,1,2,0:T(8,128)(2,1)}), bf16[128,512,2,256]{3,1,2,0:T(8,128)(2,1)}) %all-gather.3.cloned.1.call-update) | async-done | bytes 67108880 | tf_op jit(solution)/shard_map/all_gather | solution.py:13
  253.4 208.5 %while.16 = (s32[]{:T(128)}, s32[2,2,512]{2,1,0:T(2,128)S(1)}, bf16[2,512,2,256]{3,1,2,0:T(8,128)(2,1)S(1)}, s32[]{:T(128)}, s32[64,2,2,512]{3,2,1,0:T(2,128)S(1...) while((s32[]{:T(128)}, s32[2,2,512]{2,1,0:T(2,128)S(1)}, ...), condition=%wide.region_2.3_spmd.clone, body=%wide.region_0.2_spmd.clone.sunk | while | flops 543692800 | bytes 6381168 | solution.py:22
  253.5 2.3 fusion.176
  260.2 2.2 fusion.176
  263.5 2.2 fusion.176
  266.8 2.2 fusion.176
  270.1 2.2 fusion.176
  273.4 2.2 fusion.176
  276.7 2.2 fusion.176
  280.0 2.2 fusion.176
  283.4 2.2 fusion.176
  286.7 2.2 fusion.176
  290.0 2.2 fusion.176
  293.3 2.2 fusion.176
  296.6 2.2 fusion.176
  299.9 2.2 fusion.176
  303.2 2.2 fusion.176
  306.5 2.2 fusion.176
  309.8 2.2 fusion.176
  313.1 2.2 fusion.176
  316.4 2.2 fusion.176
  319.8 2.2 fusion.176
  323.1 2.2 fusion.176
  326.4 2.2 fusion.176
  329.7 2.2 fusion.176
  333.0 2.2 fusion.176
  336.3 2.2 fusion.176
  339.6 2.2 fusion.176
  342.9 2.2 fusion.176
  346.2 2.2 fusion.176
  349.5 2.2 fusion.176
  352.8 2.2 fusion.176
  356.2 2.2 fusion.176
  359.5 2.2 fusion.176
  385.9 2.2 fusion.176
  448.8 2.2 fusion.176
  464.5 3.7 fusion.18
  468.2 6.0 %all-to-all-start = ((bf16[64,4,8,512]{3,2,1,0:T(8,128)(2,1)}), bf16[64,4,8,512]{3,2,1,0:T(8,128)(2,1)S(1)}, u32[]{:S(2)}, u32[]{:S(2)}) async-start(bf16[64,4,8,512]{3,2,1,0:T(8,128)(2,1)} %bitcast.213), calls=%async_computation | async-start | bytes 4194304 | tf_op jit(solution)/shard_map/all_to_all | solution.py:120
  475.6 3.7 fusion.163
  479.3 3.6 fusion.160
  485.7 3.6 fusion.157
  489.3 3.6 fusion.156
  499.2 24.6 %all-to-all-done = bf16[64,4,8,512]{3,2,1,0:T(8,128)(2,1)S(1)} async-done(((bf16[64,4,8,512]{3,2,1,0:T(8,128)(2,1)}), bf16[64,4,8,512]{3,2,1,0:T(8,128)(2,1)S(1)}, u32[]{:S(2)}, u32[]{:S(2)}) %all-to-all-start) | async-done | bytes 2097184 | tf_op jit(solution)/shard_map/all_to_all | solution.py:120
  525.3 4.0 all-to-all-start.1
  533.3 2.3 fusion.79
  539.2 14.0 %all-to-all-done.1 = bf16[64,4,8,512]{3,2,0,1:T(8,128)(2,1)S(1)} async-done(((bf16[64,4,8,512]{3,2,0,1:T(8,128)(2,1)}), bf16[64,4,8,512]{3,2,0,1:T(8,128)(2,1)S(1)}, u32[]{:S(2)}, u32[]{:S(2)}) %all-to-all-start.1) | async-done | bytes 2097184 | tf_op jit(solution)/shard_map/all_to_all | solution.py:119
  553.2 2.7 copy.140
  (355 shorter events, 160.5 us)
Async XLA Ops:
  7.2 4.3 copy-start.5
  7.2 246.2 %all-gather.3.cloned.1.call-start = ((), (), s32[]{:S(2)}) async-start(), calls=%async_computation.2 | async-start | bytes 68157440 | tf_op jit(solution)/shard_map/all_gather | solution.py:13
  9.8 4.8 copy-start.8
  14.7 0.7 copy-start.7
  253.4 208.7 %copy-start.6 = (bf16[2,512,2,256]{3,1,2,0:T(8,128)(2,1)S(1)}, bf16[2,512,2,256]{3,1,2,0:T(8,128)(2,1)}, u32[]{:S(2)}) copy-start(bf16[2,512,2,256]{3,1,2,0:T(8,128)(2,1)} %fusion.26) | copy-start | bytes 3145732
  468.2 55.6 %all-to-all-start = ((bf16[64,4,8,512]{3,2,1,0:T(8,128)(2,1)}), bf16[64,4,8,512]{3,2,1,0:T(8,128)(2,1)S(1)}, u32[]{:S(2)}, u32[]{:S(2)}) async-start(bf16[64,4,8,512]{3,2,1,0:T(8,128)(2,1)} %bitcast.213), calls=%async_computation | async-start | bytes 4194304 | tf_op jit(solution)/shard_map/all_to_all | solution.py:120
  482.9 2.5 copy-start.3
  492.9 2.5 copy-start
  492.9 3.3 copy-start.2
  496.2 1.8 copy-start.4
  525.3 27.9 %all-to-all-start.1 = ((bf16[64,4,8,512]{3,2,0,1:T(8,128)(2,1)}), bf16[64,4,8,512]{3,2,0,1:T(8,128)(2,1)S(1)}, u32[]{:S(2)}, u32[]{:S(2)}) async-start(bf16[64,4,8,512]{3,2,0,1:T(8,128)(2,1)} %copy.116), calls=%async_computation.1 | async-start | bytes 4194304 | tf_op jit(solution)/shard_map/all_to_all | solution.py:119
  533.3 2.5 copy-start.1
Sparse Core Ops, SparseCore 0:
  11.4 241.9 all-gather.2
where the time goes:
time: 569 us; the launch traced here: 565 us
  waiting for transfers between devices  221 us (39%)
  matrix products  167 us (29%)
  other arithmetic  72.8 us (13%)
  blocking collectives  54.9 us (10%)
  local copies, waits for them, and re-layouts  20.2 us (4%)
  between operations  15.5 us (3%)
  starting transfers between devices  9.97 us (2%)
    all_gather x1, waiting for transfers between devices, carried_in(): pieces = jax.tree.map(lambda part: lax.all_gather(part, axis), value)  182 us
    dot_general x64, matrix products, compose(): jnp.einsum('phst,pthc->pshc', table.astype(jnp.bfloat16), early_rows, pre...  142 us
    reduce_sum x63, other arithmetic, compose(): jnp.sum(jnp.where(table, early_marks[..., None, :], 0), axis=-1)  57.7 us
    all_gather x1, blocking collectives, carried_in(): pieces = jax.tree.map(lambda part: lax.all_gather(part, axis), value)  54.9 us
    all_to_all x1, waiting for transfers between devices, local(): lax.all_to_all(packed, 'ctx', split_axis=0, concat_axis=0, tiled=True)  24.6 us
    sub x4, matrix products, local(): expo = jnp.where(allowed, jnp.exp(attention_scores - peak), 0.0)  14.5 us
    all_to_all x1, waiting for transfers between devices, local(): lax.all_to_all(lax.all_to_all(packed, 'ctx', split_axis=0, concat_axis=0,...  14 us
  transfers between devices with their start and end apart: 3, of which 3 were waited for; matrix products, arithmetic and copies ran while one was open for 6% of the time, Pallas kernels for 0%

commit v1 on v0

v1 whole, which is shorter than its diff:
```python
import functools, math
import jax, jax.numpy as jnp
from jax import lax
from jax.sharding import PartitionSpec as P
from jax.experimental import pallas as pl
from jax.experimental.pallas import tpu as pltpu
MESH = pl.DeviceIdType.MESH
BF = jnp.bfloat16
HEAD = 128

def lookup(table, index):
    row = lax.broadcasted_iota(jnp.int32, (8, 128), 0)
    lane = jnp.bitwise_and(index, 127)
    part = jnp.right_shift(index, 7)
    out = jnp.zeros_like(table)
    for k in range(4):
        low = jnp.broadcast_to(table[k : k + 1], (8, 128))
        high = jnp.broadcast_to(table[4 + k : 5 + k], (8, 128))
        spread = jnp.where(row < 4, low, high)
        found = jnp.take_along_axis(spread, lane, axis=1, mode="promise_in_bounds")
        out = jnp.where(part == k, found, out)
    return out

def picker(index, count):
    rows = lax.broadcasted_iota(jnp.int32, (count, 128), 0)
    return jnp.where(rows == index, 1.0, 0.0).astype(BF)

def dot(a, b):
    return jnp.dot(a, b, preferred_element_type=jnp.float32)

def k1(kv_ref, keep_ref, late_ref, latekeep_ref, in_ref, valid_ref, spans, keeps, own, owns, marks, cz, lspan, lkeep,
       ssp, ske, sow, sma, scz, rsp, rke, row_, rma, rcz, sl, rl):
    j = lax.axis_index("ctx"); x = lax.axis_index("kv")
    z = j // 8; i = lax.rem(j, 8)
    def zdev(zz): return (zz * 8 + i, x)
    def pdev(ii): return (z * 8 + ii, x)
    barrier = pltpu.get_barrier_semaphore()
    for k in range(1, 8):
        pl.semaphore_signal(barrier, inc=1, device_id=pdev(lax.rem(i + k, 8)), device_id_type=MESH)
        pl.semaphore_signal(barrier, inc=1, device_id=zdev(lax.rem(z + k, 8)), device_id_type=MESH)
    keeps[i] = keep_ref[...]
    for b in range(4):
        spans[i, b * 128 : (b + 1) * 128, :] = kv_ref[b].T
    pl.semaphore_wait(barrier, 14)
    def send(src, dst, ss, rs, dev):
        return pltpu.make_async_remote_copy(src_ref=src, dst_ref=dst, send_sem=ss, recv_sem=rs, device_id=dev, device_id_type=MESH)
    plane = []
    for k in range(1, 8):
        c = send(keeps.at[i], keeps.at[i], ske.at[k], rke.at[i], pdev(lax.rem(i + k, 8))); c.start(); plane.append(c)
    for k in range(1, 8):
        c = send(spans.at[i], spans.at[i], ssp.at[k], rsp.at[i], pdev(lax.rem(i + k, 8))); c.start(); plane.append(c)
    @pl.when(j == 62)
    def _():
        for b in range(4):
            lspan[b * 128 : (b + 1) * 128, :] = late_ref[b].T
        lkeep[...] = latekeep_ref[...]
        send(lkeep, lkeep, sl.at[0], rl.at[0], (63, x)).start()
        send(lspan, lspan, sl.at[1], rl.at[1], (63, x)).start()
    def arrive(buf, sem, k):
        pltpu.make_async_copy(buf.at[k], buf.at[k], sem.at[k]).wait()
    for k in range(1, 8):
        arrive(keeps, rke, lax.rem(i + k, 8))
    slot = lax.rem(lax.broadcasted_iota(jnp.int32, (8, 128), 0), 4) * 128 + lax.broadcasted_iota(jnp.int32, (8, 128), 1)
    pre = slot; mine = slot
    for n in range(8):
        mine = jnp.where(i == n, pre, mine)
        kept = keeps[n]
        pre = jnp.where(kept < 512, lookup(pre, jnp.minimum(kept, 511)), kept + 128 * n)
    marks[z] = pre
    for k in range(1, 8):
        @pl.when(z + k < 8)
        def _():
            send(marks.at[z], marks.at[z], sma.at[k], rma.at[z], zdev(z + k)).start()
    for k in range(1, 8):
        arrive(spans, rsp, lax.rem(i + k, 8))
    cols = pl.ds(pl.multiple_of(i * 64, 64), 64)
    head = jnp.where(i < 4, pre[0:4], pre[4:8])
    unit = jnp.concatenate([spans[n, cols, :] for n in range(8)], axis=1)
    for k in range(4):
        own[k * 64 : (k + 1) * 64, :] = dot(unit, picker(head[k : k + 1] - 512, 1024)).astype(BF)
    for k in range(1, 8):
        @pl.when(z + k < 8)
        def _():
            send(own, owns.at[z], sow.at[k], row_.at[z], zdev(z + k)).start()
    for h in range(2):
        table = jnp.concatenate([spans[n, h * 256 : (h + 1) * 256, :] for n in range(8)], axis=1)
        for k in range(4):
            in_ref[0, k, h * 256 : (h + 1) * 256, :] = dot(table, picker(mine[h * 4 + k : h * 4 + k + 1] - 512, 1024)).astype(BF)
    @pl.when(j != 63)
    def _():
        in_ref[1] = jnp.zeros((4, 512, 128), BF)
        valid_ref[1] = jnp.zeros((8, 128), jnp.int32)
    @pl.when(j == 63)
    def _():
        pltpu.make_async_copy(lkeep, lkeep, rl.at[0]).wait()
        pltpu.make_async_copy(lspan, lspan, rl.at[1]).wait()
        kept = lkeep[...]
        valid_ref[1] = jnp.where(kept >= 512, 1, 0)
        for h in range(2):
            for k in range(4):
                in_ref[1, k, h * 256 : (h + 1) * 256, :] = dot(lspan[h * 256 : (h + 1) * 256, :], picker(kept[h * 4 + k : h * 4 + k + 1] - 512, 128)).astype(BF)
    for n in range(7):
        @pl.when(n < z)
        def _():
            arrive(marks, rma, n)
    cur = jnp.full((8, 128), -1, jnp.int32)
    for n in range(7):
        m = jnp.where(n < z, marks[n], slot)
        new = jnp.where(m < 512, lookup(cur, jnp.minimum(m, 511)), n * 512 + slot)
        cur = jnp.where(n < z, new, cur)
    chead = jnp.where(i < 4, cur[0:4], cur[4:8])
    acc_ref = cz.at[i]
    acc_ref[...] = jnp.zeros((256, 128), BF)
    for n in range(7):
        @pl.when(n < z)
        def _():
            arrive(owns, row_, n)
            table = jnp.concatenate([owns[n, q * 64 : (q + 1) * 64, :] for q in range(4)], axis=1)
            for k in range(4):
                acc_ref[k * 64 : (k + 1) * 64, :] += dot(table, picker(chead[k : k + 1] - n * 512, 512)).astype(BF)
    for k in range(1, 8):
        c = send(cz.at[i], cz.at[i], scz.at[k], rcz.at[i], pdev(lax.rem(i + k, 8))); c.start(); plane.append(c)
    was = jnp.where(cur >= 0, 1, 0)
    valid_ref[0] = jnp.where(mine >= 512, 1, lookup(was, jnp.minimum(mine, 511)))
    for k in range(1, 8):
        arrive(cz, rcz, lax.rem(i + k, 8))
    for h in range(2):
        table = jnp.concatenate(
            [jnp.concatenate([cz[n, q * 64 : (q + 1) * 64, :] for q in range(4)], axis=1) for n in range(h * 4, h * 4 + 4)], axis=0
        )
        for k in range(4):
            in_ref[0, k, h * 256 : (h + 1) * 256, :] += dot(table, picker(mine[h * 4 + k : h * 4 + k + 1], 512)).astype(BF)
    for c in plane:
        c.wait_send()
    for k in range(1, 8):
        @pl.when(z + k < 8)
        def _():
            send(marks.at[z], marks.at[z], sma.at[k], rma.at[z], zdev(z + k)).wait_send()
            send(own, owns.at[z], sow.at[k], row_.at[z], zdev(z + k)).wait_send()
    @pl.when(j == 62)
    def _():
        send(lkeep, lkeep, sl.at[0], rl.at[0], (63, x)).wait_send()
        send(lspan, lspan, sl.at[1], rl.at[1], (63, x)).wait_send()

def handed_on(kv_e, keep_e, kv_l, keep_l):
    V = pltpu.VMEM; S = pltpu.SemaphoreType.DMA
    return pl.pallas_call(k1,
        out_shape=(jax.ShapeDtypeStruct((2, 4, 512, 128), BF), jax.ShapeDtypeStruct((2, 8, 128), jnp.int32)),
        in_specs=[pl.BlockSpec(memory_space=V)] * 4, out_specs=(pl.BlockSpec(memory_space=V),) * 2,
        scratch_shapes=[V((8, 512, 128), BF), V((8, 8, 128), jnp.int32), V((256, 128), BF), V((8, 256, 128), BF),
                        V((8, 8, 128), jnp.int32), V((8, 256, 128), BF), V((512, 128), BF), V((8, 128), jnp.int32)]
                       + [S((8,))] * 10 + [S((2,))] * 2,
        compiler_params=pltpu.CompilerParams(collective_id=0, has_side_effects=True, vmem_limit_bytes=32 << 20),
    )(kv_e, keep_e, kv_l, keep_l)


def placed_rows(owner_ids, capacity):
    count = owner_ids.shape[0]
    before = jnp.arange(count)[None, :] < jnp.arange(count)[:, None]
    same = owner_ids[None, :] == owner_ids[:, None]
    rank = jnp.sum(jnp.where(before & same, 1, 0), axis=1)
    return owner_ids * capacity + rank


def local(query, kv_rows, keep, dest, offsets):
    prompts, span, qwidth = query.shape
    position = lax.axis_index("ctx")
    first = offsets[0] == 0
    keep_local = keep[:, 0]
    tiles = keep_local.reshape(2, 8, 128)
    blocks = jnp.transpose(kv_rows.reshape(2, span, 4, 128), (0, 2, 1, 3))
    in_t, in_valid = handed_on(
        jnp.where(first, blocks[0], blocks[1]),
        jnp.where(first, tiles[0], tiles[1]),
        jnp.where(first, blocks[1], blocks[0]),
        jnp.where(first, tiles[1], tiles[0]),
    )
    in_t = jnp.where(first, in_t, in_t[::-1])
    in_t = jnp.transpose(in_t, (0, 2, 1, 3)).reshape(2, 2, 256, 512)
    valid = jnp.where(first, in_valid, in_valid[::-1]).reshape(2, 2, 512) > 0
    active = position >= offsets
    span_t = jnp.transpose(kv_rows.reshape(2, span, 2, 256), (0, 2, 3, 1))
    all_t = jnp.concatenate([in_t, span_t], axis=3)
    chosen = jnp.where(active[:, None, None], keep_local, jnp.arange(512, dtype=jnp.int32))
    pick = (chosen[..., None] == jnp.arange(640, dtype=jnp.int32)).astype(BF)
    outgoing = jnp.einsum("phst,phct->pshc", pick, all_t, preferred_element_type=jnp.float32).astype(BF)
    target = placed_rows(dest[:, 0], 8)
    placing = (target[None, :] == jnp.arange(2048, dtype=jnp.int32)[:, None]).astype(BF)
    packed = jnp.dot(placing, outgoing.reshape(1024, 512), preferred_element_type=jnp.float32).astype(BF)
    arrived = lax.all_to_all(packed.reshape(256, 8, 512), ("ctx", "kv"), 0, 0, tiled=True)
    owner_cache = jnp.transpose(arrived.reshape(64, 4, 8, 512), (0, 2, 1, 3)).reshape(512, 2048)
    qfive = query.reshape(2, span, 2, 8, HEAD)
    causal = jnp.arange(span)[None, :] <= jnp.arange(span)[:, None]
    scale = 1.0 / math.sqrt(HEAD)
    outputs, masses = [], []
    for prompt in range(2):
        flag = active[prompt].astype(jnp.float32)
        for head in range(2):
            table = all_t[prompt, head]
            scores = jnp.einsum("qgd,dk->gqk", qfive[prompt, :, head], table[:HEAD], preferred_element_type=jnp.float32) * scale
            seen = jnp.broadcast_to(valid[prompt, head][None, :], (span, 512))
            allowed = jnp.concatenate([seen, causal], axis=1)[None]
            scores = jnp.where(allowed, scores, -1e30)
            peak = jnp.max(scores, axis=-1, keepdims=True)
            expo = jnp.where(allowed, jnp.exp(scores - peak), 0.0)
            weights = expo / jnp.sum(expo, axis=-1, keepdims=True)
            mixed = jnp.einsum("gqk,dk->qgd", weights.astype(BF), table[HEAD:], preferred_element_type=jnp.float32)
            outputs.append((mixed * flag).astype(BF))
            masses.append(jnp.sum(weights, axis=(0, 1)) * flag)
    attention = jnp.stack(outputs).reshape(2, 2, span, 8 * HEAD).transpose(0, 2, 1, 3).reshape(2, span, qwidth)
    return (attention, jnp.stack(masses).reshape(2, 2, 640), owner_cache)


def solution(mesh):
    placed = (
        P(None, "ctx", "kv"),
        P(None, "ctx", "kv"),
        P(None, "ctx", "kv", None),
        P("ctx", None),
        P(),
    )
    return jax.shard_map(
        local,
        mesh=mesh,
        in_specs=placed,
        out_specs=(P(None, "ctx", "kv"), P(None, "kv", "ctx"), P(("ctx", "kv"), None)),
        check_vma=False,
    )
```

time: 569 us -> 128 us (0.22)
  waiting for transfers between devices: 221 us -> 21.3 us
  matrix products: 167 us -> 21.8 us
  other arithmetic: 72.8 us -> 10.9 us
  blocking collectives: 54.9 us -> 0 us
  Pallas kernels: 0 us -> 35.5 us
  between operations: 15.5 us -> 2.86 us
  starting transfers between devices: 9.97 us -> 20.6 us
    all_gather x1 -> x0, waiting for transfers between devices: 182 us -> none  [carried_in(): pieces = jax.tree.map(lambda part: lax.all_gather(part, axis), value)]
    dot_general x70 -> x6, matrix products: 152 us -> 7.18 us  [the longest x1 3.66 us: local(): jnp.dot(placing, outgoing.reshape(1024, 512), preferred_element_type=jnp....]
    reduce_sum x68 -> x5, other arithmetic: 62.8 us -> 6.17 us  [the longest x4 4.78 us: local(): masses.append(jnp.sum(weights, axis=(0, 1)) * flag)]
    all_gather x1 -> x0, blocking collectives: 54.9 us -> none  [carried_in(): pieces = jax.tree.map(lambda part: lax.all_gather(part, axis), value)]
    pallas_call x0 -> x1, Pallas kernels: none -> 35.5 us  [handed_on(): pl.pallas_call(k1, out_shape=(jax.ShapeDtypeStruct((2, 4, 512, 128), BF),...]
    all_to_all x2 -> x1, waiting for transfers between devices: 38.7 us -> 21.3 us  [local(): lax.all_to_all(packed.reshape(256, 8, 512), ('ctx', 'kv'), 0, 0, tiled=True)]
    all_to_all x2 -> x1, starting transfers between devices: 9.93 us -> 20.6 us  [local(): lax.all_to_all(packed.reshape(256, 8, 512), ('ctx', 'kv'), 0, 0, tiled=True)]
  transfers between devices with their start and end apart: 3 -> 1, of which waited for: 3 -> 1; matrix products, arithmetic and copies ran while one was open for 6% -> 21% of each run, Pallas kernels for 0% -> 0%
where the time goes in v1:
time: 128 us
  Pallas kernels  35.5 us (28%)
  matrix products  21.8 us (17%)
  waiting for transfers between devices  21.3 us (17%)
  starting transfers between devices  20.6 us (16%)
  local copies, waits for them, and re-layouts  14.6 us (11%)
  other arithmetic  10.9 us (9%)
  between operations  2.86 us (2%)
    pallas_call x1, Pallas kernels, handed_on(): pl.pallas_call(k1, out_shape=(jax.ShapeDtypeStruct((2, 4, 512, 128), BF),...  35.5 us
    all_to_all x1, waiting for transfers between devices, local(): lax.all_to_all(packed.reshape(256, 8, 512), ('ctx', 'kv'), 0, 0, tiled=True)  21.3 us
    all_to_all x1, starting transfers between devices, local(): lax.all_to_all(packed.reshape(256, 8, 512), ('ctx', 'kv'), 0, 0, tiled=True)  20.6 us
    sub x4, matrix products, local(): expo = jnp.where(allowed, jnp.exp(scores - peak), 0.0)  14.7 us
    unnamed x20, local copies, waits for them, and re-layouts  8.92 us
    reduce_sum x4, other arithmetic, local(): masses.append(jnp.sum(weights, axis=(0, 1)) * flag)  4.78 us
    dot_general x1, matrix products, local(): jnp.dot(placing, outgoing.reshape(1024, 512), preferred_element_type=jnp....  3.66 us
  transfers between devices with their start and end apart: 1, of which 1 were waited for; matrix products, arithmetic and copies ran while one was open for 21% of the time, Pallas kernels for 0%

profile of v1, /device:TPU:1, one launch (start us, length us, event | category | flops | bytes accessed | tf_op | source)
XLA Modules:
  0.0 127.5 jit_solution(4377838263634272835)
XLA Ops:
  0.6 1.4 %select_reduce_fusion = s32[1024]{0:T(1024)S(1)} fusion(s32[1024]{0:T(1024)} %bitcast.200), kind=kLoop, calls=%fused_computation.18 | loop fusion | flops 5241856 | bytes 8192 | tf_op jit(solution)/shard_map/reduce_sum | solution.py:161
  2.0 0.7 multiply_add_fusion
  2.7 0.7 broadcast_compare_fusion
  4.0 0.8 bitcast_select_fusion.8
  4.8 0.7 broadcast_select_fusion
  5.5 1.1 copy.40
  6.7 0.2 copy.41
  6.9 0.1 copy.44
  7.0 35.5 %shard_map.76 = (bf16[2,4,512,128]{3,2,1,0:T(8,128)(2,1)S(1)}, s32[2,8,128]{2,1,0:T(8,128)S(1)}) custom-call(bf16[4,128,128]{2,1,0:T(8,128)(2,1)S(1)} %get-tuple-element.12.kv_ref, s32[8,128]{1,0:T(8,128)S(1)} %select_n.91.keep_ref, bf16[4,128,128]{2,1,0:T(8,128)(2,1)S(1)} %get-tuple-element.11.late_ref, s32[8,128]{1,0:T(8,128)S(1)} %select_n.95.latekeep_ref), custom_call_target="tpu_custom_call" | custom-call | tf_op jit(solution)/shard_map/pallas_call | solution.py:147
  42.5 0.2 fusion.78
  42.7 0.8 copy.42
  43.5 0.4 reshape.139
  44.0 0.5 copy.45
  44.5 0.0 copy-start.6
  44.5 1.0 copy-done.6
  45.5 1.9 %fusion.16 = bf16[2,512,2,256]{1,3,2,0:T(8,128)(2,1)S(1)} fusion(s32[2,2,512]{2,1,0:T(2,128)S(1)} %bitcast_select_fusion.8, bf16[2,2,256,128]{2,3,1,0:T(8,128)(2,1)S(1)} %bitcast.191, bf16[2,2,256,512]{2,3,1,0:T(8,128)(2,1)S(1)} %copy.45), kind=kOutput, calls=%fused_computation.38 | convolution fusion | flops 675545088 | bytes 2367488 | tf_op jit(solution)/shard_map/phst,phct->pshc/dot_general | solution.py:186
  47.4 0.9 copy.61
  48.3 0.2 copy.80
  48.5 3.7 %fusion.14 = bf16[256,8,512]{2,1,0:T(8,128)(2,1)} fusion(bf16[1024,512]{1,0:T(8,128)(2,1)S(1)} %bitcast.190, s32[1024]{0:T(1024)S(1)} %multiply_add_fusion), kind=kOutput, calls=%fused_computation.35 | convolution fusion | flops 2150629376 | bytes 3149824 | tf_op jit(solution)/shard_map/dot_general | solution.py:189
  52.2 0.0 copy-start.5
  52.2 20.6 %all-to-all-start = ((bf16[256,8,512]{2,1,0:T(8,128)(2,1)}), bf16[256,8,512]{2,1,0:T(8,128)(2,1)S(1)}, u32[]{:S(2)}, u32[]{:S(2)}) async-start(bf16[256,8,512]{2,1,0:T(8,128)(2,1)} %fusion.14), calls=%async_computation | async-start | bytes 4194304 | tf_op jit(solution)/shard_map/all_to_all | solution.py:190
  72.8 0.7 fusion.145
  75.0 0.0 copy-done.5
  75.0 1.3 %copy.46 = bf16[2,128,2048]{1,2,0:T(8,128)(2,1)} copy(bf16[2,128,2048]{2,1,0:T(8,128)(2,1)S(1)} %copy-done.5) | data formatting | bytes 2097152 | tf_op args[0]
  76.3 1.4 %pad_add_fusion.3 = (pred[128,640]{0,1:T(8,128)(4,1)}, pred[128,640]{0,1:T(8,128)(4,1)}, pred[128,640]{0,1:T(8,128)(4,1)}, pred[128,640]{0,1:T(8,128)(4,1)S(1)}) fusion(pred[128,128]{0,1:T(8,128)(4,1)S(1)} %iota_compare_fusion.13, pred[640]{0:T(1024)(128)(4,1)S(1)} %pad.14.clone, pred[640]{0:T(1024)(128)(4,1)S(1)} %pad.12.clone, ...), kind=kLoop, calls=%fused_computation.93 | loop fusion | flops 327680 | bytes 346624 | tf_op jit(solution)/shard_map/concatenate | solution.py:202
  77.7 3.8 %fusion.152 = (f32[8,128]{1,0:T(8,128)S(1)}, f32[8,128,640]{1,2,0:T(8,128)}) fusion(pred[128,640]{0,1:T(8,128)(4,1)} %get-tuple-element.14, bf16[2,128,2,8,128]{1,4,3,2,0:T(8,128)(2,1)} %bitcast.186, bf16[2,2,256,512]{2,3,1,0:T(8,128)(2,1)} %copy-done.6, bf16[2,2,256,128]{2,3,1,0:T(8,128)(2,1)S(1)} %bitcast.192), kind=kOutput, calls=%fused_computation.161 | convolution fusion | flops 171377280 | bytes 4362240 | tf_op jit(solution)/shard_map/sub | solution.py:205
  81.5 0.0 copy-done.7
  81.5 3.6 %fusion.155 = (f32[8,128]{1,0:T(8,128)S(1)}, f32[8,128,640]{1,2,0:T(8,128)}) fusion(pred[128,640]{0,1:T(8,128)(4,1)} %get-tuple-element.13, bf16[2,128,2,8,128]{1,4,3,2,0:T(8,128)(2,1)} %bitcast.187, bf16[2,2,256,512]{2,3,1,0:T(8,128)(2,1)S(1)} %copy-done.7, bf16[2,2,256,128]{2,3,1,0:T(8,128)(2,1)S(1)} %bitcast.193), kind=kOutput, calls=%fused_computation.162 | convolution fusion | flops 171377280 | bytes 4362240 | tf_op jit(solution)/shard_map/sub | solution.py:205
  85.2 2.1 %fusion.75 = f32[640]{0:T(1024)S(1)} fusion(f32[8,128,640]{1,2,0:T(8,128)} %get-tuple-element.26, f32[8,128]{1,0:T(8,128)S(1)} %get-tuple-element.25), kind=kLoop, calls=%fused_computation.85 | loop fusion | flops 1310080 | bytes 2628096 | tf_op jit(solution)/shard_map/reduce_sum | solution.py:209
  87.3 0.4 copy-done.1
  87.7 0.3 fusion.74
  88.0 3.6 %fusion.149 = (f32[8,128]{1,0:T(8,128)S(1)}, f32[8,128,640]{1,2,0:T(8,128)}) fusion(pred[128,640]{0,1:T(8,128)(4,1)} %get-tuple-element.15, bf16[2,128,2,8,128]{1,4,3,2,0:T(8,128)(2,1)} %bitcast.188, bf16[2,2,256,512]{2,3,1,0:T(8,128)(2,1)S(1)} %copy-done.7, bf16[2,2,256,128]{2,3,1,0:T(8,128)(2,1)S(1)} %bitcast.194), kind=kOutput, calls=%fused_computation.160 | convolution fusion | flops 171377280 | bytes 4362240 | tf_op jit(solution)/shard_map/sub | solution.py:205
  91.6 3.6 %fusion.146 = (f32[8,128]{1,0:T(8,128)S(1)}, f32[8,128,640]{1,2,0:T(8,128)}) fusion(pred[128,640]{0,1:T(8,128)(4,1)S(1)} %get-tuple-element.16, bf16[2,128,2,8,128]{1,4,3,2,0:T(8,128)(2,1)} %bitcast.189, bf16[2,2,256,512]{2,3,1,0:T(8,128)(2,1)S(1)} %copy-done.7, bf16[2,2,256,128]{2,3,1,0:T(8,128)(2,1)S(1)} %bitcast.195), kind=kOutput, calls=%fused_computation.159 | convolution fusion | flops 171377280 | bytes 4362240 | tf_op jit(solution)/shard_map/sub | solution.py:205
  95.2 2.1 %fusion.76 = f32[640]{0:T(1024)S(1)} fusion(f32[8,128,640]{1,2,0:T(8,128)} %get-tuple-element.24, f32[8,128]{1,0:T(8,128)S(1)} %get-tuple-element.23), kind=kLoop, calls=%fused_computation.86 | loop fusion | flops 1310080 | bytes 2628096 | tf_op jit(solution)/shard_map/reduce_sum | solution.py:209
  97.3 0.4 copy-done.3
  97.7 0.3 fusion.77
  98.0 0.5 copy-done.4
  98.5 0.4 fusion.67
  98.9 1.3 %copy-done = f32[8,128,640]{1,2,0:T(8,128)S(1)} copy-done((f32[8,128,640]{1,2,0:T(8,128)S(1)}, f32[8,128,640]{1,2,0:T(8,128)}, u32[]{:S(2)}) %copy-start) | copy-done | bytes 2621464
  100.3 0.4 fusion.64
  100.7 1.3 %copy-done.2 = f32[8,128,640]{1,2,0:T(8,128)S(1)} copy-done((f32[8,128,640]{1,2,0:T(8,128)S(1)}, f32[8,128,640]{1,2,0:T(8,128)}, u32[]{:S(2)}) %copy-start.2) | copy-done | bytes 2621464
  102.0 0.4 fusion.61
  102.4 0.4 fusion.70
  102.8 0.1 pad_maximum_fusion.2
  103.0 1.3 %copy.75 = bf16[2,128,2048]{2,1,0:T(8,128)(2,1)} copy(bf16[2,128,2048]{1,2,0:T(8,128)(2,1)S(1)} %bitcast.181) | data formatting | bytes 2097152 | tf_op jit(solution)/shard_map/reshape | solution.py:210
  104.3 0.6 reshape.144
  104.9 21.3 %all-to-all-done = bf16[256,8,512]{2,1,0:T(8,128)(2,1)S(1)} async-done(((bf16[256,8,512]{2,1,0:T(8,128)(2,1)}), bf16[256,8,512]{2,1,0:T(8,128)(2,1)S(1)}, u32[]{:S(2)}, u32[]{:S(2)}) %all-to-all-start) | async-done | bytes 2097184 | tf_op jit(solution)/shard_map/all_to_all | solution.py:190
  126.2 1.3 %copy.82 = bf16[512,2048]{1,0:T(8,128)(2,1)} copy(bf16[512,2048]{1,0:T(8,128)(2,1)S(1)} %bitcast.180) | data formatting | bytes 4194304
  (24 shorter events, 0.2 us)
Async XLA Ops:
  44.5 1.0 copy-start.6
  52.2 22.8 %copy-start.5 = (bf16[2,128,2048]{2,1,0:T(8,128)(2,1)S(1)}, bf16[2,128,2048]{2,1,0:T(8,128)(2,1)}, u32[]{:S(2)}) copy-start(bf16[2,128,2048]{2,1,0:T(8,128)(2,1)} %param.5) | copy-start | bytes 3145732
  52.2 74.0 %all-to-all-start = ((bf16[256,8,512]{2,1,0:T(8,128)(2,1)}), bf16[256,8,512]{2,1,0:T(8,128)(2,1)S(1)}, u32[]{:S(2)}, u32[]{:S(2)}) async-start(bf16[256,8,512]{2,1,0:T(8,128)(2,1)} %fusion.14), calls=%async_computation | async-start | bytes 4194304 | tf_op jit(solution)/shard_map/all_to_all | solution.py:190
  77.7 3.8 %copy-start.7 = (bf16[2,2,256,512]{2,3,1,0:T(8,128)(2,1)S(1)}, bf16[2,2,256,512]{2,3,1,0:T(8,128)(2,1)}, u32[]{:S(2)}) copy-start(bf16[2,2,256,512]{2,3,1,0:T(8,128)(2,1)} %copy-done.6) | copy-start | bytes 3145732
  85.1 2.5 %copy-start.1 = (f32[8,128,640]{1,2,0:T(8,128)S(1)}, f32[8,128,640]{1,2,0:T(8,128)}, u32[]{:S(2)}) copy-start(f32[8,128,640]{1,2,0:T(8,128)} %get-tuple-element.28) | copy-start | bytes 7864324
  95.2 2.5 %copy-start.3 = (f32[8,128,640]{1,2,0:T(8,128)S(1)}, f32[8,128,640]{1,2,0:T(8,128)}, u32[]{:S(2)}) copy-start(f32[8,128,640]{1,2,0:T(8,128)} %get-tuple-element.22) | copy-start | bytes 7864324
  95.2 3.3 %copy-start.4 = (f32[8,128,640]{1,2,0:T(8,128)S(1)}, f32[8,128,640]{1,2,0:T(8,128)}, u32[]{:S(2)}) copy-start(f32[8,128,640]{1,2,0:T(8,128)} %get-tuple-element.24) | copy-start | bytes 7864324
  98.5 1.7 %copy-start = (f32[8,128,640]{1,2,0:T(8,128)S(1)}, f32[8,128,640]{1,2,0:T(8,128)}, u32[]{:S(2)}) copy-start(f32[8,128,640]{1,2,0:T(8,128)} %get-tuple-element.26) | copy-start | bytes 7864324
  100.3 1.7 %copy-start.2 = (f32[8,128,640]{1,2,0:T(8,128)S(1)}, f32[8,128,640]{1,2,0:T(8,128)}, u32[]{:S(2)}) copy-start(f32[8,128,640]{1,2,0:T(8,128)} %get-tuple-element.28) | copy-start | bytes 7864324

commit v2 on v1

v2 whole, which is shorter than its diff:
```python
import math

import jax
import jax.numpy as jnp
from jax import lax
from jax.experimental import pallas as pl
from jax.experimental.pallas import tpu as pltpu
from jax.sharding import PartitionSpec as P

MESH = pl.DeviceIdType.MESH
BF = jnp.bfloat16
HEAD = 128


def lookup(table, index):
    row = lax.broadcasted_iota(jnp.int32, (8, 128), 0)
    lane = jnp.bitwise_and(index, 127)
    part = jnp.right_shift(index, 7)
    out = jnp.zeros_like(table)
    for k in range(4):
        low = jnp.broadcast_to(table[k : k + 1], (8, 128))
        high = jnp.broadcast_to(table[4 + k : 5 + k], (8, 128))
        spread = jnp.where(row < 4, low, high)
        found = jnp.take_along_axis(spread, lane, axis=1, mode="promise_in_bounds")
        out = jnp.where(part == k, found, out)
    return out


def picker(index, count):
    rows = lax.broadcasted_iota(jnp.int32, (count, 128), 0)
    return jnp.where(rows == index, 1.0, 0.0).astype(BF)


def dot(a, b):
    return jnp.dot(a, b, preferred_element_type=jnp.float32)


def dot_t(a, b):
    return lax.dot_general(a, b, (((1,), (1,)), ((), ())), preferred_element_type=jnp.float32)


def lanes(parts):
    return jnp.concatenate(parts, axis=1)


def inverse(kept, values):
    row = lax.broadcasted_iota(jnp.int32, (16, 128), 0)
    total = jnp.zeros((16, 640), jnp.float32)
    for k in range(4):
        value = values[k : k + 1] + 1
        high = jnp.broadcast_to(jnp.right_shift(value, 6), (16, 128))
        low = jnp.broadcast_to(jnp.bitwise_and(value, 63), (16, 128))
        digits = jnp.where(row == 0, high, jnp.where(row == 1, low, 0)).astype(jnp.float32).astype(BF)
        total = total + dot_t(digits, picker(kept[k : k + 1], 640))
    return (total[0:1] * 64.0 + total[1:2]).astype(jnp.int32) - 1


def half(rows, which):
    return jnp.where(which == 0, rows[0:4], rows[4:8])


def kernel(offs, kv, q, keep, goal, attn, mass, recv, spans, keeps, own, owns, marks, cz, late, cache, valid, tab, metas, tabl, obuf,
           s_sp, s_ke, s_ow, s_ma, s_cz, r_sp, r_ke, r_ow, r_ma, r_cz, s_la, r_la,
           s_up, r_up, s_dn, r_dn, s_mu, r_mu, s_md, r_md, s_lu, r_lu, s_ld, r_ld, s_ex, r_ex, s_lo):
    j = lax.axis_index("ctx")
    x = lax.axis_index("kv")
    z = j // 8
    i = lax.rem(j, 8)
    y = i // 2
    c = lax.rem(i, 2)
    me = i * 4 + x
    early = jnp.where(offs[0] == 0, 0, 1)

    def zdev(n):
        return (n * 8 + i, x)

    def pdev(n):
        return (z * 8 + n, x)

    def mdev(n):
        return (z * 8 + n // 4, lax.rem(n, 4))

    barrier = pltpu.get_barrier_semaphore()

    @pl.loop(1, 32)
    def _(k):
        pl.semaphore_signal(barrier, inc=1, device_id=mdev(lax.rem(me + k, 32)), device_id_type=MESH)

    @pl.loop(1, 8)
    def _(k):
        pl.semaphore_signal(barrier, inc=1, device_id=zdev(lax.rem(z + k, 8)), device_id_type=MESH)

    keeps[i, 0:8, :] = keep[early]
    keeps[i, 8:16, :] = keep[1 - early]
    keeps[i, 16:20, :] = goal[early]
    keeps[i, 20:24, :] = goal[1 - early]
    for b in range(4):
        spans[i, b * 128 : (b + 1) * 128, :] = kv[early, b].T
    final_pair = j >= 62

    @pl.when(final_pair)
    def _():
        for b in range(4):
            late[c, b * 128 : (b + 1) * 128, :] = kv[1 - early, b].T

    pl.semaphore_wait(barrier, 38)

    def send(src, dst, ss, rs, dev):
        return pltpu.make_async_remote_copy(
            src_ref=src, dst_ref=dst, send_sem=ss, recv_sem=rs, device_id=dev, device_id_type=MESH
        )

    def took(view, sem):
        pltpu.make_async_copy(view, view, sem).wait()

    def arrive(buf, sem, k):
        took(buf.at[k], sem.at[k])

    def late_copy():
        return send(late.at[c], late.at[c], s_la, r_la, pdev(7 - c))

    waits = []
    for k in range(1, 8):
        copy = send(keeps.at[i], keeps.at[i], s_ke.at[k], r_ke.at[i], pdev(lax.rem(i + k, 8)))
        copy.start()
        waits.append(copy)
    for k in range(1, 8):
        copy = send(spans.at[i], spans.at[i], s_sp.at[k], r_sp.at[i], pdev(lax.rem(i + k, 8)))
        copy.start()
        waits.append(copy)

    @pl.when(final_pair)
    def _():
        late_copy().start()

    for k in range(1, 8):
        arrive(keeps, r_ke, lax.rem(i + k, 8))
    slot = lax.rem(lax.broadcasted_iota(jnp.int32, (8, 128), 0), 4) * 128 + lax.broadcasted_iota(jnp.int32, (8, 128), 1)
    pre, mine = slot, slot
    for n in range(8):
        mine = jnp.where(i == n, pre, mine)
        kept = keeps[n, 0:8, :]
        pre = jnp.where(kept < 512, lookup(pre, jnp.minimum(kept, 511)), kept + 128 * n)
    marks[z] = pre

    def marks_copy(k):
        return send(marks.at[z], marks.at[z], s_ma.at[k], r_ma.at[z], zdev(z + k))

    def own_copy(k):
        return send(own, owns.at[z], s_ow.at[k], r_ow.at[z], zdev(z + k))

    for k in range(1, 8):
        @pl.when(z + k < 8)
        def _():
            marks_copy(k).start()

    first, second = i - c, i - c + 1
    goal0 = keeps[first, 16:20, :]
    goal1 = inverse(half(keeps[second, 0:8, :], c), keeps[second, 16:20, :])
    metas[z, 0:4, :] = goal0
    metas[z, 4:8, :] = jnp.full((4, 128), -1, jnp.int32)
    for k in range(5):
        metas[z, 8 + k : 9 + k, :] = goal1[:, k * 128 : (k + 1) * 128]
    metas[z, 13:16, :] = jnp.full((3, 128), -1, jnp.int32)

    @pl.when(final_pair)
    def _():
        kept0 = half(keeps[first, 8:16, :], c)
        kept1 = half(keeps[second, 8:16, :], c)
        out1 = inverse(kept1, keeps[second, 20:24, :])
        back = jnp.concatenate([out1[:, k * 128 : (k + 1) * 128] for k in range(4)], axis=0)
        metas[z, 5:6, :] = inverse(kept0, keeps[first, 20:24, :])[:, 512:640]
        metas[z, 13:14, :] = inverse(kept0, back)[:, 512:640]
        metas[z, 14:15, :] = out1[:, 512:640]

    for k in range(1, 8):
        arrive(spans, r_sp, lax.rem(i + k, 8))
    cols = pl.ds(pl.multiple_of(i * 64, 64), 64)
    head = jnp.where(i < 4, pre[0:4], pre[4:8])
    unit = lanes([spans[n, cols, :] for n in range(8)])
    for k in range(4):
        own[k * 64 : (k + 1) * 64, :] = dot(unit, picker(head[k : k + 1] - 512, 1024)).astype(BF)
    for k in range(1, 8):
        @pl.when(z + k < 8)
        def _():
            own_copy(k).start()

    for h in range(2):
        table = lanes([spans[n, h * 256 : (h + 1) * 256, :] for n in range(8)])
        for k in range(4):
            cache[0, k, h * 256 : (h + 1) * 256, :] = dot(table, picker(mine[h * 4 + k : h * 4 + k + 1] - 512, 1024)).astype(BF)

    for n in range(7):
        @pl.when(n < z)
        def _():
            arrive(marks, r_ma, n)
    cur = jnp.full((8, 128), -1, jnp.int32)
    for n in range(7):
        m = jnp.where(n < z, marks[n], slot)
        new = jnp.where(m < 512, lookup(cur, jnp.minimum(m, 511)), n * 512 + slot)
        cur = jnp.where(n < z, new, cur)
    chead = jnp.where(i < 4, cur[0:4], cur[4:8])
    part = cz.at[i]
    part[...] = jnp.zeros((256, 128), BF)
    for n in range(7):
        @pl.when(n < z)
        def _():
            arrive(owns, r_ow, n)
            table = lanes([owns[n, p * 64 : (p + 1) * 64, :] for p in range(4)])
            for k in range(4):
                part[k * 64 : (k + 1) * 64, :] += dot(table, picker(chead[k : k + 1] - n * 512, 512)).astype(BF)
    for k in range(1, 8):
        copy = send(cz.at[i], cz.at[i], s_cz.at[k], r_cz.at[i], pdev(lax.rem(i + k, 8)))
        copy.start()
        waits.append(copy)
    was = jnp.where(cur >= 0, 1, 0)
    valid[0] = jnp.where(mine >= 512, 1, lookup(was, jnp.minimum(mine, 511)))

    @pl.when(final_pair)
    def _():
        took(late.at[1 - c], r_la)
        for h in range(2):
            tabl[h] = late[h, pl.ds(pl.multiple_of(c * 256, 256), 256), :]

    for k in range(1, 8):
        arrive(cz, r_cz, lax.rem(i + k, 8))
    for h in range(2):
        table = jnp.concatenate(
            [lanes([cz[n, p * 64 : (p + 1) * 64, :] for p in range(4)]) for n in range(h * 4, h * 4 + 4)], axis=0
        )
        for k in range(4):
            cache[0, k, h * 256 : (h + 1) * 256, :] += dot(table, picker(mine[h * 4 + k : h * 4 + k + 1], 512)).astype(BF)

    tab[z, 4] = spans[second, pl.ds(pl.multiple_of(c * 256, 256), 256), :]

    @pl.when(c == 1)
    def _():
        for k in range(4):
            tab[z, k] = cache[0, k, 256:512, :]

    @pl.when(c == 0)
    def _():
        table = lanes([cache[0, k, 0:256, :] for k in range(4)] + [spans[i, 0:256, :]])
        kept = keeps[i, 0:8, :]
        for k in range(4):
            tab[z, k] = dot(table, picker(kept[k : k + 1], 640)).astype(BF)

    above, below = zdev(lax.rem(z + 1, 8)), zdev(lax.rem(z + 7, 8))

    def up(s):
        o = lax.rem(z + 9 - s, 8)
        view = tab.at[o, pl.ds(0, 5 if s < 4 else 2)]
        return o, [
            send(metas.at[o], metas.at[o], s_mu.at[s], r_mu.at[s], above),
            send(view, view, s_up.at[s], r_up.at[s], above),
        ], send(tabl, tabl, s_lu, r_lu, above)

    def down(s):
        o = lax.rem(z + s - 1, 8)
        view = tab.at[o, pl.ds(0, 5)] if s < 4 else tab.at[o, pl.ds(2, 3)]
        parts = [send(view, view, s_dn.at[s], r_dn.at[s], below)]
        if s < 4:
            parts.append(send(metas.at[o], metas.at[o], s_md.at[s], r_md.at[s], below))
        return o, parts, send(tabl, tabl, s_ld, r_ld, below) if s < 4 else None

    def pass_on(s):
        o, parts, extra = up(s)
        for copy in parts:
            copy.start()

        @pl.when((o == 7) & (y == 3))
        def _():
            extra.start()

        o, parts, extra = down(s)
        for copy in parts:
            copy.start()
        if s < 4:
            @pl.when((o == 7) & (y == 3))
            def _():
                extra.start()

    def passed(s):
        for make in (up, down):
            o, parts, extra = make(s)
            for copy in parts:
                copy.wait_send()
            if s < 4 or make is up:
                @pl.when((o == 7) & (y == 3))
                def _():
                    extra.wait_send()

    def receive(s):
        o = lax.rem(z + 8 - s, 8)
        took(metas.at[o], r_mu.at[s])
        took(tab.at[o, pl.ds(0, 5 if s < 4 else 2)], r_up.at[s])

        @pl.when((o == 7) & (y == 3))
        def _():
            took(tabl, r_lu)

        o = lax.rem(z + s, 8)
        took(tab.at[o, pl.ds(0, 5)] if s < 4 else tab.at[o, pl.ds(2, 3)], r_dn.at[s])
        if s < 4:
            took(metas.at[o], r_md.at[s])

            @pl.when((o == 7) & (y == 3))
            def _():
                took(tabl, r_ld)

    def exchange(o, n):
        dst = recv.at[pl.ds(x * 4 + c * 2, 2), pl.ds(pl.multiple_of((o * 4 + y) * 16, 16), 16), :]
        return send(obuf.at[o, :, pl.ds(pl.multiple_of(n * 16, 16), 16), :], dst, s_ex.at[o], r_ex.at[o], mdev(n))

    def keep_local(o):
        dst = recv.at[pl.ds(x * 4 + c * 2, 2), pl.ds(pl.multiple_of((o * 4 + y) * 16, 16), 16), :]
        return pltpu.make_async_copy(obuf.at[o, :, pl.ds(pl.multiple_of(me * 16, 16), 16), :], dst, s_lo.at[o])

    line = lax.broadcasted_iota(jnp.int32, (512, 128), 0)
    place = z * 256 + jnp.right_shift(line, 4) * 8 + jnp.bitwise_and(line, 7)
    later = jnp.bitwise_and(line, 8) > 0

    def hit(o, k):
        wanted = jnp.where(later, metas[o, 8 + k : 9 + k, :], metas[o, k : k + 1, :])
        return jnp.where(wanted == place, 1.0, 0.0).astype(BF)

    def hand_out(o):
        rows = dot_t(lanes([hit(o, k) for k in range(5)]), lanes([tab[o, k] for k in range(5)])).astype(BF)
        obuf[o, 0] = rows[:, 0:128]
        obuf[o, 1] = rows[:, 128:256]

        @pl.when((o == 7) & (y == 3))
        def _():
            rows = dot_t(lanes([hit(o, k) for k in (5, 6)]), lanes([tabl[k] for k in range(2)])).astype(BF)
            obuf[o, 0] += rows[:, 0:128]
            obuf[o, 1] += rows[:, 128:256]

        @pl.loop(1, 32)
        def _(k):
            exchange(o, lax.rem(me + k, 32)).start()

        keep_local(o).start()

    own_tokens = lax.broadcasted_iota(jnp.int32, (128, 128), 1) <= lax.broadcasted_iota(jnp.int32, (128, 128), 0)

    def attend(p, h, span_t):
        def chunk(at):
            return lanes([cache[p, k, at : at + 128, :] for k in range(4)] + [span_t[at : at + 128, :]])

        keys, values = chunk(h * 256), chunk(h * 256 + 128)
        seen = lanes([jnp.broadcast_to(valid[p, h * 4 + k : h * 4 + k + 1, :], (128, 128)) for k in range(4)]) > 0
        near = own_tokens
        prompt = early if p == 0 else 1 - early
        scale = 1.0 / math.sqrt(HEAD)

        def one(g, total):
            scores = dot(q[prompt, h * 8 + g], keys) * scale
            old = jnp.where(seen, scores[:, 0:512], -1e30)
            new = jnp.where(near, scores[:, 512:640], -1e30)
            peak = jnp.maximum(jnp.max(old, axis=1, keepdims=True), jnp.max(new, axis=1, keepdims=True))
            expo = lanes([jnp.where(seen, jnp.exp(old - peak), 0.0), jnp.where(near, jnp.exp(new - peak), 0.0)])
            weights = expo * (1.0 / jnp.sum(expo, axis=1, keepdims=True))
            attn[p, h * 8 + g] = dot_t(weights.astype(BF), values).astype(BF)
            return total + jnp.sum(weights.reshape(16, 8, 640), axis=0)

        total = lax.fori_loop(0, 8, one, jnp.zeros((8, 640), jnp.float32))
        mass[p * 2 + h : p * 2 + h + 1, :] = jnp.sum(total, axis=0, keepdims=True)

    def attend_late():
        @pl.when(final_pair)
        def _():
            cache[1] = jnp.zeros((4, 512, 128), BF)
            valid[1] = jnp.zeros((8, 128), jnp.int32)

            @pl.when(c == 1)
            def _():
                kept = keeps[first, 8:16, :]
                valid[1] = jnp.where(kept >= 512, 1, 0)
                for h in range(2):
                    for k in range(4):
                        cache[1, k, h * 256 : (h + 1) * 256, :] = dot(
                            late[0, h * 256 : (h + 1) * 256, :], picker(kept[h * 4 + k : h * 4 + k + 1] - 512, 128)
                        ).astype(BF)

            for h in range(2):
                attend(1, h, late.at[c])

        @pl.when(jnp.logical_not(final_pair))
        def _():
            attn[1] = jnp.zeros((16, 128, 128), BF)
            mass[2:4, :] = jnp.zeros((2, 640), jnp.float32)

    pass_on(1)
    hand_out(z)
    attend(0, 0, spans.at[i])
    for s in (1, 2, 3):
        receive(s)
        pass_on(s + 1)
        hand_out(lax.rem(z + 8 - s, 8))
        hand_out(lax.rem(z + s, 8))
        if s == 1:
            attend(0, 1, spans.at[i])
        if s == 2:
            attend_late()
    receive(4)
    hand_out(lax.rem(z + 4, 8))

    for copy in waits:
        copy.wait_send()
    for k in range(1, 8):
        @pl.when(z + k < 8)
        def _():
            marks_copy(k).wait_send()
            own_copy(k).wait_send()

    @pl.when(final_pair)
    def _():
        late_copy().wait_send()

    for s in (1, 2, 3, 4):
        passed(s)

    @pl.loop(0, 8)
    def _(o):
        keep_local(o).wait()
        took(obuf.at[o, :, pl.ds(0, 496), :], s_ex.at[o])
        took(recv.at[pl.ds(0, 2), pl.ds(0, 496), :], r_ex.at[o])


def whole(offsets, kv, q, keep, goal):
    V, D = pltpu.VMEM, pltpu.SemaphoreType.DMA
    vmem = pl.BlockSpec(memory_space=V)
    return pl.pallas_call(
        kernel,
        out_shape=(
            jax.ShapeDtypeStruct((2, 16, 128, 128), BF),
            jax.ShapeDtypeStruct((4, 640), jnp.float32),
            jax.ShapeDtypeStruct((16, 512, 128), BF),
        ),
        in_specs=[pl.BlockSpec(memory_space=pltpu.SMEM)] + [vmem] * 4,
        out_specs=(vmem,) * 3,
        scratch_shapes=[
            V((8, 512, 128), BF),
            V((8, 24, 128), jnp.int32),
            V((256, 128), BF),
            V((8, 256, 128), BF),
            V((8, 8, 128), jnp.int32),
            V((8, 256, 128), BF),
            V((2, 512, 128), BF),
            V((2, 4, 512, 128), BF),
            V((2, 8, 128), jnp.int32),
            V((8, 5, 256, 128), BF),
            V((8, 16, 128), jnp.int32),
            V((2, 256, 128), BF),
            V((8, 2, 512, 128), BF),
        ]
        + [D((8,))] * 10
        + [D] * 2
        + [D((5,))] * 8
        + [D] * 4
        + [D((8,))] * 3,
        compiler_params=pltpu.CompilerParams(collective_id=0, has_side_effects=True, vmem_limit_bytes=40 << 20),
    )(offsets, kv, q, keep, goal)


def placed_rows(owner_ids, capacity):
    count = owner_ids.shape[0]
    before = jnp.arange(count)[None, :] < jnp.arange(count)[:, None]
    same = owner_ids[None, :] == owner_ids[:, None]
    rank = jnp.sum(jnp.where(before & same, 1, 0), axis=1)
    return owner_ids * capacity + rank


def local(query, kv_rows, keep, dest, offsets):
    span = query.shape[1]
    first = offsets[0] == 0
    attn, mass, owned = whole(
        offsets,
        jnp.transpose(kv_rows.reshape(2, span, 4, 128), (0, 2, 1, 3)),
        jnp.transpose(query.reshape(2, span, 16, 128), (0, 2, 1, 3)),
        keep.reshape(2, 8, 128),
        placed_rows(dest[:, 0], 8).reshape(2, 4, 128),
    )
    attn = jnp.where(first, attn, attn[::-1])
    attention = jnp.transpose(attn, (0, 2, 1, 3)).reshape(query.shape)
    mass = mass.reshape(2, 2, 640)
    row_scores = jnp.where(first, mass, mass[::-1])
    owner_cache = jnp.transpose(owned, (1, 0, 2)).reshape(512, 2048)
    return (attention, row_scores, owner_cache)


def solution(mesh):
    placed = (
        P(None, "ctx", "kv"),
        P(None, "ctx", "kv"),
        P(None, "ctx", "kv", None),
        P("ctx", None),
        P(),
    )
    return jax.shard_map(
        local,
        mesh=mesh,
        in_specs=placed,
        out_specs=(P(None, "ctx", "kv"), P(None, "kv", "ctx"), P(("ctx", "kv"), None)),
        check_vma=False,
    )
```

time: 128 us -> 115 us (0.90)
  Pallas kernels: 35.5 us -> 95.2 us
  matrix products: 21.8 us -> 0 us
  waiting for transfers between devices: 21.3 us -> 0 us
  starting transfers between devices: 20.6 us -> 0 us
  other arithmetic: 10.9 us -> 2.97 us
  between operations: 2.86 us -> 1.34 us
    pallas_call x1, Pallas kernels: 35.5 us -> 95.2 us  [whole(): pl.pallas_call(kernel, out_shape=(jax.ShapeDtypeStruct((2, 16, 128, 128),...]
    all_to_all x1 -> x0, waiting for transfers between devices: 21.3 us -> none  [local(): lax.all_to_all(packed.reshape(256, 8, 512), ('ctx', 'kv'), 0, 0, tiled=True)]
    all_to_all x1 -> x0, starting transfers between devices: 20.6 us -> none  [local(): lax.all_to_all(packed.reshape(256, 8, 512), ('ctx', 'kv'), 0, 0, tiled=True)]
    sub x4 -> x0, matrix products: 14.7 us -> none  [local(): expo = jnp.where(allowed, jnp.exp(scores - peak), 0.0)]
    dot_general x6 -> x0, matrix products: 7.18 us -> none  [the longest x1 3.66 us: local(): jnp.dot(placing, outgoing.reshape(1024, 512), preferred_element_type=jnp....]
    reduce_sum x4 -> x0, other arithmetic: 4.78 us -> none  [local(): masses.append(jnp.sum(weights, axis=(0, 1)) * flag)]
    transpose x1 -> x2, local copies, waits for them, and re-layouts: 0.81 us -> 3.91 us  [the longest x1 2.6 us: local(): owner_cache = jnp.transpose(owned, (1, 0, 2)).reshape(512, 2048)]
    reshape x6 -> x4, local copies, waits for them, and re-layouts: 3.23 us -> 1.6 us  [the longest x1 0.71 us: local(): keep.reshape(2, 8, 128)]
  transfers between devices with their start and end apart: 1 -> 0, of which waited for: 1 -> 0; matrix products, arithmetic and copies ran while one was open for 21% -> 0% of each run, Pallas kernels for 0% -> 0%
where the time goes in v2:
time: 115 us; the launch traced here: 114 us
  Pallas kernels  95.2 us (83%)
  local copies, waits for them, and re-layouts  14.4 us (13%)
  other arithmetic  2.97 us (3%)
  between operations  1.34 us (1%)
    pallas_call x1, Pallas kernels, whole(): pl.pallas_call(kernel, out_shape=(jax.ShapeDtypeStruct((2, 16, 128, 128),...  95.2 us
    unnamed x6, local copies, waits for them, and re-layouts  8.91 us
    transpose x1, local copies, waits for them, and re-layouts, local(): owner_cache = jnp.transpose(owned, (1, 0, 2)).reshape(512, 2048)  2.6 us

profile of v2, /device:TPU:1, one launch (start us, length us, event | category | flops | bytes accessed | tf_op | source)
XLA Modules:
  0.0 114.0 jit_solution(2056710594497723632)
XLA Ops:
  1.3 1.4 %select_reduce_fusion = s32[1024]{0:T(1024)S(1)} fusion(s32[1024]{0:T(1024)} %bitcast.24), kind=kLoop, calls=%fused_computation | loop fusion | flops 5241856 | bytes 8192 | tf_op jit(solution)/shard_map/reduce_sum | solution.py:470
  2.7 0.7 broadcast_multiply_fusion
  3.4 0.7 reshape.34.keep
  4.1 1.1 copy.16
  5.2 0.2 copy.17
  5.4 0.0 copy-start
  5.4 1.6 %copy.18 = bf16[2,128,2048]{1,2,0:T(8,128)(2,1)S(1)} copy(bf16[2,128,2048]{2,1,0:T(8,128)(2,1)} %param.5) | data formatting | bytes 2097152 | tf_op args[0]
  7.0 0.7 copy.19
  7.7 0.0 copy-done
  7.7 95.2 %shard_map.76 = (bf16[2,16,128,128]{3,2,1,0:T(8,128)(2,1)S(1)}, f32[4,640]{1,0:T(4,128)S(1)}, bf16[16,512,128]{2,1,0:T(8,128)(2,1)S(1)}) custom-call(s32[2]{0:T(128)S(1)} %copy-done, bf16[2,4,128,128]{3,2,1,0:T(8,128)(2,1)S(1)} %bitcast.16, bf16[2,16,128,128]{3,2,1,0:T(8,128)(2,1)S(1)} %bitcast.14, s32[2,8,128]{2,1,0:T(8,128)S(1)} %reshape.34.keep, ...), custom_call_target="tpu_custom_call" | custom-call | tf_op jit(solution)/shard_map/pallas_call | solution.py:433
  103.0 0.3 fusion.1
  103.3 1.3 %copy.20 = bf16[2,128,16,128]{1,3,2,0:T(8,128)(2,1)} copy(bf16[2,128,16,128]{3,1,2,0:T(8,128)(2,1)S(1)} %fusion.1) | data formatting | bytes 2097152 | tf_op jit(solution)/shard_map/transpose | solution.py:485
  104.6 2.3 %copy.22 = bf16[2,128,2048]{2,1,0:T(8,128)(2,1)} copy(bf16[2,128,2048]{1,2,0:T(8,128)(2,1)} %bitcast.19) | data formatting | bytes 2097152
  106.9 0.6 reverse_select_fusion.1
  107.5 2.6 %copy.21 = bf16[512,16,128]{0,2,1:T(8,128)(2,1)} copy(bf16[512,16,128]{2,0,1:T(8,128)(2,1)S(1)} %bitcast.15) | data formatting | bytes 4194304 | tf_op jit(solution)/shard_map/transpose | solution.py:488
  110.1 3.9 %copy.23 = bf16[512,2048]{1,0:T(8,128)(2,1)} copy(bf16[512,2048]{0,1:T(8,128)(2,1)} %bitcast.18) | data formatting | bytes 4194304
  (2 shorter events, 0.0 us)
Async XLA Ops:
  5.4 2.3 %copy-start = (s32[2]{0:T(128)S(1)}, s32[2]{0:T(128)}, u32[]{:S(2)}) copy-start(s32[2]{0:T(128)} %offs.1) | copy-start | bytes 28

commit v3 on v2

--- a/solution.py
+++ b/solution.py
@@ -59,7 +59,7 @@
     return jnp.where(which == 0, rows[0:4], rows[4:8])
 
 
-def kernel(offs, kv, q, keep, goal, attn, mass, recv, spans, keeps, own, owns, marks, cz, late, cache, valid, tab, metas, tabl, obuf,
+def kernel(offs, kv, q, keep, goal, attn, mass, owned, recv, spans, keeps, own, owns, marks, cz, late, cache, valid, tab, metas, tabl, obuf,
            s_sp, s_ke, s_ow, s_ma, s_cz, r_sp, r_ke, r_ow, r_ma, r_cz, s_la, r_la,
            s_up, r_up, s_dn, r_dn, s_mu, r_mu, s_md, r_md, s_lu, r_lu, s_ld, r_ld, s_ex, r_ex, s_lo):
     j = lax.axis_index("ctx")
@@ -90,18 +90,22 @@
     def _(k):
         pl.semaphore_signal(barrier, inc=1, device_id=zdev(lax.rem(z + k, 8)), device_id_type=MESH)
 
-    keeps[i, 0:8, :] = keep[early]
-    keeps[i, 8:16, :] = keep[1 - early]
+    for p in range(2):
+        lists = keep[early if p == 0 else 1 - early]
+        for h in range(2):
+            for k in range(4):
+                at = p * 8 + h * 4 + k
+                keeps[i, at : at + 1, :] = lists[h : h + 1, k * 128 : (k + 1) * 128]
     keeps[i, 16:20, :] = goal[early]
     keeps[i, 20:24, :] = goal[1 - early]
     for b in range(4):
-        spans[i, b * 128 : (b + 1) * 128, :] = kv[early, b].T
+        spans[i, b * 128 : (b + 1) * 128, :] = kv[early, :, b].reshape(128, 128).T
     final_pair = j >= 62
 
     @pl.when(final_pair)
     def _():
         for b in range(4):
-            late[c, b * 128 : (b + 1) * 128, :] = kv[1 - early, b].T
+            late[c, b * 128 : (b + 1) * 128, :] = kv[1 - early, :, b].reshape(128, 128).T
 
     pl.semaphore_wait(barrier, 38)
 
@@ -247,66 +251,72 @@
 
     above, below = zdev(lax.rem(z + 1, 8)), zdev(lax.rem(z + 7, 8))
 
-    def up(s):
-        o = lax.rem(z + 9 - s, 8)
-        view = tab.at[o, pl.ds(0, 5 if s < 4 else 2)]
-        return o, [
-            send(metas.at[o], metas.at[o], s_mu.at[s], r_mu.at[s], above),
-            send(view, view, s_up.at[s], r_up.at[s], above),
-        ], send(tabl, tabl, s_lu, r_lu, above)
-
-    def down(s):
-        o = lax.rem(z + s - 1, 8)
-        view = tab.at[o, pl.ds(0, 5)] if s < 4 else tab.at[o, pl.ds(2, 3)]
-        parts = [send(view, view, s_dn.at[s], r_dn.at[s], below)]
+    WAYS = (("up", 1), ("down", -1))
+
+    def chunks(way, s):
+        return range(5) if s < 4 else (range(2) if way == "up" else range(2, 5))
+
+    def origin(way, s):
+        return lax.rem(z + 8 - s, 8) if way == "up" else lax.rem(z + s, 8)
+
+    def chunk_copy(way, s, k):
+        o = origin(way, s - 1)
+        ss, rs, to = (s_up, r_up, above) if way == "up" else (s_dn, r_dn, below)
+        return send(tab.at[o, k], tab.at[o, k], ss.at[s * 5 + k], rs.at[s * 5 + k], to)
+
+    def metas_copy(way, s):
+        o = origin(way, s - 1)
+        ss, rs, to = (s_mu, r_mu, above) if way == "up" else (s_md, r_md, below)
+        return send(metas.at[o], metas.at[o], ss.at[s], rs.at[s], to)
+
+    def tabl_copy(way):
+        ss, rs, to = (s_lu, r_lu, above) if way == "up" else (s_ld, r_ld, below)
+        return send(tabl, tabl, ss, rs, to)
+
+    def has_late(way, s):
+        return (origin(way, s) == 7) & (y == 3)
+
+    def goes(way, s):
+        return s <= (4 if way == "up" else 3)
+
+    def lead(s):
+        for way, _ in WAYS:
+            if goes(way, s):
+                metas_copy(way, s).start()
+
+                @pl.when(has_late(way, s - 1))
+                def _():
+                    tabl_copy(way).start()
+
+    def receive(s, tasks):
+        for way, _ in WAYS:
+            if goes(way, s):
+                took(metas.at[origin(way, s)], (r_mu if way == "up" else r_md).at[s])
+
+                @pl.when(has_late(way, s))
+                def _():
+                    took(tabl, r_lu if way == "up" else r_ld)
         if s < 4:
-            parts.append(send(metas.at[o], metas.at[o], s_md.at[s], r_md.at[s], below))
-        return o, parts, send(tabl, tabl, s_ld, r_ld, below) if s < 4 else None
-
-    def pass_on(s):
-        o, parts, extra = up(s)
-        for copy in parts:
-            copy.start()
-
-        @pl.when((o == 7) & (y == 3))
-        def _():
-            extra.start()
-
-        o, parts, extra = down(s)
-        for copy in parts:
-            copy.start()
-        if s < 4:
-            @pl.when((o == 7) & (y == 3))
-            def _():
-                extra.start()
+            lead(s + 1)
+        for k in range(5):
+            for way, _ in WAYS:
+                if k in chunks(way, s):
+                    took(tab.at[origin(way, s), k], (r_up if way == "up" else r_dn).at[s * 5 + k])
+                if s < 4 and k in chunks(way, s + 1):
+                    chunk_copy(way, s + 1, k).start()
+            if k < len(tasks):
+                tasks[k]()
 
     def passed(s):
-        for make in (up, down):
-            o, parts, extra = make(s)
-            for copy in parts:
-                copy.wait_send()
-            if s < 4 or make is up:
-                @pl.when((o == 7) & (y == 3))
+        for way, _ in WAYS:
+            for k in chunks(way, s):
+                chunk_copy(way, s, k).wait_send()
+            if goes(way, s):
+                metas_copy(way, s).wait_send()
+
+                @pl.when(has_late(way, s - 1))
                 def _():
-                    extra.wait_send()
-
-    def receive(s):
-        o = lax.rem(z + 8 - s, 8)
-        took(metas.at[o], r_mu.at[s])
-        took(tab.at[o, pl.ds(0, 5 if s < 4 else 2)], r_up.at[s])
-
-        @pl.when((o == 7) & (y == 3))
-        def _():
-            took(tabl, r_lu)
-
-        o = lax.rem(z + s, 8)
-        took(tab.at[o, pl.ds(0, 5)] if s < 4 else tab.at[o, pl.ds(2, 3)], r_dn.at[s])
-        if s < 4:
-            took(metas.at[o], r_md.at[s])
-
-            @pl.when((o == 7) & (y == 3))
-            def _():
-                took(tabl, r_ld)
+                    tabl_copy(way).wait_send()
 
     def exchange(o, n):
         dst = recv.at[pl.ds(x * 4 + c * 2, 2), pl.ds(pl.multiple_of((o * 4 + y) * 16, 16), 16), :]
@@ -354,17 +364,26 @@
         scale = 1.0 / math.sqrt(HEAD)
 
         def one(g, total):
-            scores = dot(q[prompt, h * 8 + g], keys) * scale
+            scores = dot(q[prompt, :, h * 8 + g].reshape(128, 128), keys) * scale
             old = jnp.where(seen, scores[:, 0:512], -1e30)
             new = jnp.where(near, scores[:, 512:640], -1e30)
             peak = jnp.maximum(jnp.max(old, axis=1, keepdims=True), jnp.max(new, axis=1, keepdims=True))
             expo = lanes([jnp.where(seen, jnp.exp(old - peak), 0.0), jnp.where(near, jnp.exp(new - peak), 0.0)])
             weights = expo * (1.0 / jnp.sum(expo, axis=1, keepdims=True))
-            attn[p, h * 8 + g] = dot_t(weights.astype(BF), values).astype(BF)
+            mixed = dot_t(weights.astype(BF), values)
+            at = pl.ds(pl.multiple_of((h * 8 + g) * 128, 128), 128)
+            for n in range(2):
+                part = jnp.where(prompt == n, mixed, 0.0)
+                if p == 1:
+                    part = part + attn[n, :, at].astype(jnp.float32)
+                attn[n, :, at] = part.astype(BF)
             return total + jnp.sum(weights.reshape(16, 8, 640), axis=0)
 
         total = lax.fori_loop(0, 8, one, jnp.zeros((8, 640), jnp.float32))
-        mass[p * 2 + h : p * 2 + h + 1, :] = jnp.sum(total, axis=0, keepdims=True)
+        total = jnp.sum(total, axis=0, keepdims=True)
+        for n in range(2):
+            part = jnp.where(prompt == n, total, 0.0)
+            mass[n, h : h + 1, :] = part + mass[n, h : h + 1, :] if p == 1 else part
 
     def attend_late():
         @pl.when(final_pair)
@@ -385,25 +404,20 @@
             for h in range(2):
                 attend(1, h, late.at[c])
 
-        @pl.when(jnp.logical_not(final_pair))
-        def _():
-            attn[1] = jnp.zeros((16, 128, 128), BF)
-            mass[2:4, :] = jnp.zeros((2, 640), jnp.float32)
-
-    pass_on(1)
+    lead(1)
+    for k in range(5):
+        for way, _ in WAYS:
+            chunk_copy(way, 1, k).start()
+
+    def hand(way, s):
+        return lambda: hand_out(origin(way, s))
+
     hand_out(z)
-    attend(0, 0, spans.at[i])
-    for s in (1, 2, 3):
-        receive(s)
-        pass_on(s + 1)
-        hand_out(lax.rem(z + 8 - s, 8))
-        hand_out(lax.rem(z + s, 8))
-        if s == 1:
-            attend(0, 1, spans.at[i])
-        if s == 2:
-            attend_late()
-    receive(4)
-    hand_out(lax.rem(z + 4, 8))
+    receive(1, [lambda: attend(0, 0, spans.at[i])])
+    receive(2, [hand("up", 1), hand("down", 1), lambda: attend(0, 1, spans.at[i])])
+    receive(3, [hand("up", 2), hand("down", 2), attend_late])
+    receive(4, [hand("up", 3), hand("down", 3)])
+    hand_out(origin("up", 4))
 
     for copy in waits:
         copy.wait_send()
@@ -420,11 +434,14 @@
     for s in (1, 2, 3, 4):
         passed(s)
 
-    @pl.loop(0, 8)
-    def _(o):
+    for s, way in ((0, "up"), (1, "up"), (1, "down"), (2, "up"), (2, "down"), (3, "up"), (3, "down"), (4, "up")):
+        o = origin(way, s)
         keep_local(o).wait()
         took(obuf.at[o, :, pl.ds(0, 496), :], s_ex.at[o])
         took(recv.at[pl.ds(0, 2), pl.ds(0, 496), :], r_ex.at[o])
+        rows = pl.ds(pl.multiple_of(o * 64, 64), 64)
+        for b in range(16):
+            owned[rows, b * 128 : (b + 1) * 128] = recv[b, rows, :]
 
 
 def whole(offsets, kv, q, keep, goal):
@@ -433,13 +450,14 @@
     return pl.pallas_call(
         kernel,
         out_shape=(
-            jax.ShapeDtypeStruct((2, 16, 128, 128), BF),
-            jax.ShapeDtypeStruct((4, 640), jnp.float32),
-            jax.ShapeDtypeStruct((16, 512, 128), BF),
+            jax.ShapeDtypeStruct((2, 128, 2048), BF),
+            jax.ShapeDtypeStruct((2, 2, 640), jnp.float32),
+            jax.ShapeDtypeStruct((512, 2048), BF),
         ),
         in_specs=[pl.BlockSpec(memory_space=pltpu.SMEM)] + [vmem] * 4,
         out_specs=(vmem,) * 3,
         scratch_shapes=[
+            V((16, 512, 128), BF),
             V((8, 512, 128), BF),
             V((8, 24, 128), jnp.int32),
             V((256, 128), BF),
@@ -456,7 +474,8 @@
         ]
         + [D((8,))] * 10
         + [D] * 2
-        + [D((5,))] * 8
+        + [D((25,))] * 4
+        + [D((5,))] * 4
         + [D] * 4
         + [D((8,))] * 3,
         compiler_params=pltpu.CompilerParams(collective_id=0, has_side_effects=True, vmem_limit_bytes=40 << 20),
@@ -471,22 +490,19 @@
     return owner_ids * capacity + rank
 
 
+def tiled(rows):
+    prompts, count, width = rows.shape
+    return jnp.transpose(rows.reshape(prompts, count // 8, 8, width // 128, 128), (0, 1, 3, 2, 4))
+
+
 def local(query, kv_rows, keep, dest, offsets):
-    span = query.shape[1]
-    first = offsets[0] == 0
-    attn, mass, owned = whole(
+    return whole(
         offsets,
-        jnp.transpose(kv_rows.reshape(2, span, 4, 128), (0, 2, 1, 3)),
-        jnp.transpose(query.reshape(2, span, 16, 128), (0, 2, 1, 3)),
-        keep.reshape(2, 8, 128),
+        tiled(kv_rows),
+        tiled(query),
+        keep[:, 0],
         placed_rows(dest[:, 0], 8).reshape(2, 4, 128),
     )
-    attn = jnp.where(first, attn, attn[::-1])
-    attention = jnp.transpose(attn, (0, 2, 1, 3)).reshape(query.shape)
-    mass = mass.reshape(2, 2, 640)
-    row_scores = jnp.where(first, mass, mass[::-1])
-    owner_cache = jnp.transpose(owned, (1, 0, 2)).reshape(512, 2048)
-    return (attention, row_scores, owner_cache)
 
 
 def solution(mesh):

time: 115 us -> 100 us (0.87)
  local copies, waits for them, and re-layouts: 14.4 us -> 6.41 us
  Pallas kernels: 95.2 us -> 90.5 us
    pallas_call x1, Pallas kernels: 95.2 us -> 90.5 us  [whole(): pl.pallas_call(kernel, out_shape=(jax.ShapeDtypeStruct((2, 128, 2048), BF...]
    transpose x2 -> x0, local copies, waits for them, and re-layouts: 3.91 us -> none  [the longest x1 2.6 us: local(): owner_cache = jnp.transpose(owned, (1, 0, 2)).reshape(512, 2048)]
    unnamed x6 -> x11, local copies, waits for them, and re-layouts: 8.91 us -> 6.41 us
    reshape x4 -> x0, local copies, waits for them, and re-layouts: 1.6 us -> none  [the longest x1 0.71 us: local(): keep.reshape(2, 8, 128)]
where the time goes in v3:
time: 100 us; the launch traced here: 99.7 us
  Pallas kernels  90.5 us (90%)
  local copies, waits for them, and re-layouts  6.41 us (6%)
  other arithmetic  2.09 us (2%)
    pallas_call x1, Pallas kernels, whole(): pl.pallas_call(kernel, out_shape=(jax.ShapeDtypeStruct((2, 128, 2048), BF...  90.5 us
    unnamed x11, local copies, waits for them, and re-layouts  6.41 us

profile of v3, /device:TPU:1, one launch (start us, length us, event | category | flops | bytes accessed | tf_op | source)
XLA Modules:
  0.0 99.7 jit_solution(5158970558572177424)
XLA Ops:
  0.6 1.4 %select_reduce_fusion = s32[1024]{0:T(1024)S(1)} fusion(s32[1024]{0:T(1024)} %bitcast.15), kind=kLoop, calls=%fused_computation | loop fusion | flops 5241856 | bytes 8192 | tf_op jit(solution)/shard_map/reduce_sum | solution.py:489
  2.0 0.7 broadcast_multiply_fusion
  2.7 0.0 copy-start
  2.7 1.2 %copy-done = bf16[2,128,2048]{2,1,0:T(8,128)(2,1)S(1)} copy-done((bf16[2,128,2048]{2,1,0:T(8,128)(2,1)S(1)}, bf16[2,128,2048]{2,1,0:T(8,128)(2,1)}, u32[]{:S(2)}) %copy-start) | copy-done | bytes 1048600
  3.9 0.0 copy-start.1
  3.9 0.9 copy-done.1
  4.9 0.0 copy-start.2
  4.9 0.7 copy-done.2
  5.6 0.0 copy-start.3
  5.6 0.7 copy-done.3
  6.3 90.5 %shard_map.76 = (bf16[2,128,2048]{2,1,0:T(8,128)(2,1)S(1)}, f32[2,2,640]{2,1,0:T(2,128)S(1)}, bf16[512,2048]{1,0:T(8,128)(2,1)S(1)}) custom-call(s32[2]{0:T(128)S(1)} %copy-done.3, bf16[2,16,4,8,128]{4,3,2,1,0:T(8,128)(2,1)S(1)} %bitcast.11, bf16[2,16,16,8,128]{4,3,2,1,0:T(8,128)(2,1)S(1)} %bitcast.10, s32[2,2,512]{2,1,0:T(2,128)S(1)} %bitcast.12, ...), custom_call_target="tpu_custom_call" | custom-call | tf_op jit(solution)/shard_map/pallas_call | solution.py:450
  96.8 1.0 copy.11
  97.7 0.6 copy.12
  98.3 1.3 %copy.13 = bf16[512,2048]{1,0:T(8,128)(2,1)} copy(bf16[512,2048]{1,0:T(8,128)(2,1)S(1)} %get-tuple-element.8) | data formatting | bytes 4194304
  (1 shorter events, 0.0 us)
Async XLA Ops:
  2.7 1.2 %copy-start = (bf16[2,128,2048]{2,1,0:T(8,128)(2,1)S(1)}, bf16[2,128,2048]{2,1,0:T(8,128)(2,1)}, u32[]{:S(2)}) copy-start(bf16[2,128,2048]{2,1,0:T(8,128)(2,1)} %param.5) | copy-start | bytes 3145732
  3.9 0.9 copy-start.1
  4.9 0.7 copy-start.2
  5.6 0.7 copy-start.3

commit v4 on v3

--- a/solution.py
+++ b/solution.py
@@ -59,9 +59,9 @@
     return jnp.where(which == 0, rows[0:4], rows[4:8])
 
 
-def kernel(offs, kv, q, keep, goal, attn, mass, owned, recv, spans, keeps, own, owns, marks, cz, late, cache, valid, tab, metas, tabl, obuf,
+def kernel(offs, kv, q, keep, dest, attn, mass, owned, recv, spans, keeps, units, goals, own, owns, marks, cz, late, cache, valid, tab, metas, tabl, obuf,
            s_sp, s_ke, s_ow, s_ma, s_cz, r_sp, r_ke, r_ow, r_ma, r_cz, s_la, r_la,
-           s_up, r_up, s_dn, r_dn, s_mu, r_mu, s_md, r_md, s_lu, r_lu, s_ld, r_ld, s_ex, r_ex, s_lo):
+           s_up, r_up, s_dn, r_dn, s_lu, r_lu, s_ld, r_ld, s_ex, r_ex, s_lo, s_un, r_un, s_me, r_me, r_c4, s_c4, s_go, r_go):
     j = lax.axis_index("ctx")
     x = lax.axis_index("kv")
     z = j // 8
@@ -77,6 +77,9 @@
     def pdev(n):
         return (z * 8 + n, x)
 
+    def pair(n, core):
+        return (n * 8 + y * 2 + core, x)
+
     def mdev(n):
         return (z * 8 + n // 4, lax.rem(n, 4))
 
@@ -88,7 +91,8 @@
 
     @pl.loop(1, 8)
     def _(k):
-        pl.semaphore_signal(barrier, inc=1, device_id=zdev(lax.rem(z + k, 8)), device_id_type=MESH)
+        for n in range(2):
+            pl.semaphore_signal(barrier, inc=1, device_id=pair(lax.rem(z + k, 8), n), device_id_type=MESH)
 
     for p in range(2):
         lists = keep[early if p == 0 else 1 - early]
@@ -96,8 +100,6 @@
             for k in range(4):
                 at = p * 8 + h * 4 + k
                 keeps[i, at : at + 1, :] = lists[h : h + 1, k * 128 : (k + 1) * 128]
-    keeps[i, 16:20, :] = goal[early]
-    keeps[i, 20:24, :] = goal[1 - early]
     for b in range(4):
         spans[i, b * 128 : (b + 1) * 128, :] = kv[early, :, b].reshape(128, 128).T
     final_pair = j >= 62
@@ -107,7 +109,9 @@
         for b in range(4):
             late[c, b * 128 : (b + 1) * 128, :] = kv[1 - early, :, b].reshape(128, 128).T
 
-    pl.semaphore_wait(barrier, 38)
+    cols = pl.ds(pl.multiple_of(i * 64, 64), 64)
+    units[i] = spans[i, cols, :]
+    pl.semaphore_wait(barrier, 45)
 
     def send(src, dst, ss, rs, dev):
         return pltpu.make_async_remote_copy(
@@ -126,6 +130,11 @@
     waits = []
     for k in range(1, 8):
         copy = send(keeps.at[i], keeps.at[i], s_ke.at[k], r_ke.at[i], pdev(lax.rem(i + k, 8)))
+        copy.start()
+        waits.append(copy)
+    for k in range(1, 8):
+        n = lax.rem(i + k, 8)
+        copy = send(spans.at[i, pl.ds(pl.multiple_of(n * 64, 64), 64), :], units.at[i], s_un.at[k], r_un.at[i], pdev(n))
         copy.start()
         waits.append(copy)
     for k in range(1, 8):
@@ -158,9 +167,43 @@
         def _():
             marks_copy(k).start()
 
+    for k in range(1, 8):
+        arrive(units, r_un, lax.rem(i + k, 8))
+    head = jnp.where(i < 4, pre[0:4], pre[4:8])
+    unit = lanes([units[n] for n in range(8)])
+    for k in range(4):
+        own[k * 64 : (k + 1) * 64, :] = dot(unit, picker(head[k : k + 1] - 512, 1024)).astype(BF)
+    for k in range(1, 8):
+        @pl.when(z + k < 8)
+        def _():
+            own_copy(k).start()
+
+    owners = dest[...]
+    side = lax.broadcasted_iota(jnp.int32, (128, 128), 0) < lax.broadcasted_iota(jnp.int32, (128, 128), 1)
+    earlier = jnp.where(side, 1.0, 0.0).astype(BF)
+    count = jnp.zeros((256, 1), jnp.float32)
+    for n in range(8):
+        named = picker(owners[n : n + 1], 256)
+        before = dot(named, earlier) + count
+        named = named.astype(jnp.float32)
+        rank = jnp.sum(named * before, axis=0, keepdims=True)
+        count = count + jnp.sum(named, axis=1, keepdims=True)
+        goals[c, n : n + 1, :] = owners[n : n + 1] * 8 + rank.astype(jnp.int32)
     first, second = i - c, i - c + 1
-    goal0 = keeps[first, 16:20, :]
-    goal1 = inverse(half(keeps[second, 0:8, :], c), keeps[second, 16:20, :])
+    copy = send(goals.at[c], goals.at[c], s_go, r_go, pdev(first + 1 - c))
+    copy.start()
+    waits.append(copy)
+
+    for k in range(1, 8):
+        arrive(spans, r_sp, lax.rem(i + k, 8))
+    for h in range(2):
+        table = lanes([spans[n, h * 256 : (h + 1) * 256, :] for n in range(8)])
+        for k in range(4):
+            cache[0, k, h * 256 : (h + 1) * 256, :] = dot(table, picker(mine[h * 4 + k : h * 4 + k + 1] - 512, 1024)).astype(BF)
+
+    took(goals.at[1 - c], r_go)
+    goal0 = half(goals[0], early)
+    goal1 = inverse(half(keeps[second, 0:8, :], c), half(goals[1], early))
     metas[z, 0:4, :] = goal0
     metas[z, 4:8, :] = jnp.full((4, 128), -1, jnp.int32)
     for k in range(5):
@@ -171,28 +214,16 @@
     def _():
         kept0 = half(keeps[first, 8:16, :], c)
         kept1 = half(keeps[second, 8:16, :], c)
-        out1 = inverse(kept1, keeps[second, 20:24, :])
+        out1 = inverse(kept1, half(goals[1], 1 - early))
         back = jnp.concatenate([out1[:, k * 128 : (k + 1) * 128] for k in range(4)], axis=0)
-        metas[z, 5:6, :] = inverse(kept0, keeps[first, 20:24, :])[:, 512:640]
+        metas[z, 5:6, :] = inverse(kept0, half(goals[0], 1 - early))[:, 512:640]
         metas[z, 13:14, :] = inverse(kept0, back)[:, 512:640]
         metas[z, 14:15, :] = out1[:, 512:640]
 
     for k in range(1, 8):
-        arrive(spans, r_sp, lax.rem(i + k, 8))
-    cols = pl.ds(pl.multiple_of(i * 64, 64), 64)
-    head = jnp.where(i < 4, pre[0:4], pre[4:8])
-    unit = lanes([spans[n, cols, :] for n in range(8)])
-    for k in range(4):
-        own[k * 64 : (k + 1) * 64, :] = dot(unit, picker(head[k : k + 1] - 512, 1024)).astype(BF)
-    for k in range(1, 8):
-        @pl.when(z + k < 8)
-        def _():
-            own_copy(k).start()
-
-    for h in range(2):
-        table = lanes([spans[n, h * 256 : (h + 1) * 256, :] for n in range(8)])
-        for k in range(4):
-            cache[0, k, h * 256 : (h + 1) * 256, :] = dot(table, picker(mine[h * 4 + k : h * 4 + k + 1] - 512, 1024)).astype(BF)
+        copy = send(metas.at[z], metas.at[z], s_me.at[k], r_me.at[z], zdev(lax.rem(z + k, 8)))
+        copy.start()
+        waits.append(copy)
 
     for n in range(7):
         @pl.when(n < z)
@@ -217,6 +248,19 @@
         copy = send(cz.at[i], cz.at[i], s_cz.at[k], r_cz.at[i], pdev(lax.rem(i + k, 8)))
         copy.start()
         waits.append(copy)
+
+    def span_copies():
+        return [
+            send(spans.at[i, n * 256 : (n + 1) * 256, :], tab.at[z, 4], s_c4.at[k * 2 + n], r_c4.at[z], pair(lax.rem(z + k, 8), n))
+            for k in range(1, 8)
+            for n in range(2)
+        ]
+
+    @pl.when(c == 1)
+    def _():
+        for copy in span_copies():
+            copy.start()
+
     was = jnp.where(cur >= 0, 1, 0)
     valid[0] = jnp.where(mine >= 512, 1, lookup(was, jnp.minimum(mine, 511)))
 
@@ -254,7 +298,7 @@
     WAYS = (("up", 1), ("down", -1))
 
     def chunks(way, s):
-        return range(5) if s < 4 else (range(2) if way == "up" else range(2, 5))
+        return range(4) if s < 4 else (range(2) if way == "up" else range(2, 4))
 
     def origin(way, s):
         return lax.rem(z + 8 - s, 8) if way == "up" else lax.rem(z + s, 8)
@@ -264,11 +308,6 @@
         ss, rs, to = (s_up, r_up, above) if way == "up" else (s_dn, r_dn, below)
         return send(tab.at[o, k], tab.at[o, k], ss.at[s * 5 + k], rs.at[s * 5 + k], to)
 
-    def metas_copy(way, s):
-        o = origin(way, s - 1)
-        ss, rs, to = (s_mu, r_mu, above) if way == "up" else (s_md, r_md, below)
-        return send(metas.at[o], metas.at[o], ss.at[s], rs.at[s], to)
-
     def tabl_copy(way):
         ss, rs, to = (s_lu, r_lu, above) if way == "up" else (s_ld, r_ld, below)
         return send(tabl, tabl, ss, rs, to)
@@ -282,8 +321,6 @@
     def lead(s):
         for way, _ in WAYS:
             if goes(way, s):
-                metas_copy(way, s).start()
-
                 @pl.when(has_late(way, s - 1))
                 def _():
                     tabl_copy(way).start()
@@ -291,14 +328,12 @@
     def receive(s, tasks):
         for way, _ in WAYS:
             if goes(way, s):
-                took(metas.at[origin(way, s)], (r_mu if way == "up" else r_md).at[s])
-
                 @pl.when(has_late(way, s))
                 def _():
                     took(tabl, r_lu if way == "up" else r_ld)
         if s < 4:
             lead(s + 1)
-        for k in range(5):
+        for k in range(4):
             for way, _ in WAYS:
                 if k in chunks(way, s):
                     took(tab.at[origin(way, s), k], (r_up if way == "up" else r_dn).at[s * 5 + k])
@@ -312,8 +347,6 @@
             for k in chunks(way, s):
                 chunk_copy(way, s, k).wait_send()
             if goes(way, s):
-                metas_copy(way, s).wait_send()
-
                 @pl.when(has_late(way, s - 1))
                 def _():
                     tabl_copy(way).wait_send()
@@ -405,19 +438,24 @@
                 attend(1, h, late.at[c])
 
     lead(1)
-    for k in range(5):
+    for k in range(4):
         for way, _ in WAYS:
             chunk_copy(way, 1, k).start()
 
+    def hand_in(o):
+        arrive(metas, r_me, o)
+        took(tab.at[o, 4], r_c4.at[o])
+        hand_out(o)
+
     def hand(way, s):
-        return lambda: hand_out(origin(way, s))
+        return lambda: hand_in(origin(way, s))
 
     hand_out(z)
     receive(1, [lambda: attend(0, 0, spans.at[i])])
     receive(2, [hand("up", 1), hand("down", 1), lambda: attend(0, 1, spans.at[i])])
     receive(3, [hand("up", 2), hand("down", 2), attend_late])
     receive(4, [hand("up", 3), hand("down", 3)])
-    hand_out(origin("up", 4))
+    hand_in(origin("up", 4))
 
     for copy in waits:
         copy.wait_send()
@@ -426,6 +464,11 @@
         def _():
             marks_copy(k).wait_send()
             own_copy(k).wait_send()
+
+    @pl.when(c == 1)
+    def _():
+        for copy in span_copies():
+            copy.wait_send()
 
     @pl.when(final_pair)
     def _():
@@ -444,7 +487,7 @@
             owned[rows, b * 128 : (b + 1) * 128] = recv[b, rows, :]
 
 
-def whole(offsets, kv, q, keep, goal):
+def whole(offsets, kv, q, keep, dest):
     V, D = pltpu.VMEM, pltpu.SemaphoreType.DMA
     vmem = pl.BlockSpec(memory_space=V)
     return pl.pallas_call(
@@ -459,7 +502,9 @@
         scratch_shapes=[
             V((16, 512, 128), BF),
             V((8, 512, 128), BF),
-            V((8, 24, 128), jnp.int32),
+            V((8, 16, 128), jnp.int32),
+            V((8, 64, 128), BF),
+            V((2, 8, 128), jnp.int32),
             V((256, 128), BF),
             V((8, 256, 128), BF),
             V((8, 8, 128), jnp.int32),
@@ -475,19 +520,12 @@
         + [D((8,))] * 10
         + [D] * 2
         + [D((25,))] * 4
-        + [D((5,))] * 4
         + [D] * 4
-        + [D((8,))] * 3,
+        + [D((8,))] * 8
+        + [D((16,))]
+        + [D] * 2,
         compiler_params=pltpu.CompilerParams(collective_id=0, has_side_effects=True, vmem_limit_bytes=40 << 20),
-    )(offsets, kv, q, keep, goal)
-
-
-def placed_rows(owner_ids, capacity):
-    count = owner_ids.shape[0]
-    before = jnp.arange(count)[None, :] < jnp.arange(count)[:, None]
-    same = owner_ids[None, :] == owner_ids[:, None]
-    rank = jnp.sum(jnp.where(before & same, 1, 0), axis=1)
-    return owner_ids * capacity + rank
+    )(offsets, kv, q, keep, dest)
 
 
 def tiled(rows):
@@ -501,7 +539,7 @@
         tiled(kv_rows),
         tiled(query),
         keep[:, 0],
-        placed_rows(dest[:, 0], 8).reshape(2, 4, 128),
+        dest.reshape(8, 128),
     )
 
 

time: 100 us -> 94.3 us (0.943)
  the two profiles are of different devices: /device:TPU:1 before, /device:TPU:225 now
where the time goes in v4:
time: 94.3 us; the launch traced here: 94.1 us
  Pallas kernels  86.4 us (92%)
  local copies, waits for them, and re-layouts  7.09 us (8%)
    pallas_call x1, Pallas kernels, whole(): pl.pallas_call(kernel, out_shape=(jax.ShapeDtypeStruct((2, 128, 2048), BF...  86.4 us
    unnamed x13, local copies, waits for them, and re-layouts  7.09 us

profile of v4, /device:TPU:225, one launch (start us, length us, event | category | flops | bytes accessed | tf_op | source)
XLA Modules:
  0.0 94.1 jit_solution(10057034089968613596)
XLA Ops:
  0.6 0.0 copy-start
  0.6 1.2 %copy-done = bf16[2,128,2048]{2,1,0:T(8,128)(2,1)S(1)} copy-done((bf16[2,128,2048]{2,1,0:T(8,128)(2,1)S(1)}, bf16[2,128,2048]{2,1,0:T(8,128)(2,1)}, u32[]{:S(2)}) %copy-start) | copy-done | bytes 1048600
  1.9 0.0 copy-start.1
  1.9 0.9 %copy-done.1 = bf16[2,128,512]{2,1,0:T(8,128)(2,1)S(1)} copy-done((bf16[2,128,512]{2,1,0:T(8,128)(2,1)S(1)}, bf16[2,128,512]{2,1,0:T(8,128)(2,1)}, u32[]{:S(2)}) %copy-start.1) | copy-done | bytes 262168
  2.8 0.0 copy-start.2
  2.8 0.7 copy-done.2
  3.5 0.0 copy-start.3
  3.5 0.7 copy-done.3
  4.2 0.0 copy-start.4
  4.2 0.7 copy-done.4
  4.8 86.4 %shard_map.76 = (bf16[2,128,2048]{2,1,0:T(8,128)(2,1)S(1)}, f32[2,2,640]{2,1,0:T(2,128)S(1)}, bf16[512,2048]{1,0:T(8,128)(2,1)S(1)}) custom-call(s32[2]{0:T(128)S(1)} %copy-done.4, bf16[2,16,4,8,128]{4,3,2,1,0:T(8,128)(2,1)S(1)} %bitcast.9, bf16[2,16,16,8,128]{4,3,2,1,0:T(8,128)(2,1)S(1)} %bitcast.8, s32[2,2,512]{2,1,0:T(2,128)S(1)} %bitcast.10, ...), custom_call_target="tpu_custom_call" | custom-call | tf_op jit(solution)/shard_map/pallas_call | solution.py:493
  91.2 1.0 %copy.11 = bf16[2,128,2048]{2,1,0:T(8,128)(2,1)} copy(bf16[2,128,2048]{2,1,0:T(8,128)(2,1)S(1)} %get-tuple-element.6) | data formatting | bytes 2097152
  92.2 0.6 copy.12
  92.8 1.3 %copy.13 = bf16[512,2048]{1,0:T(8,128)(2,1)} copy(bf16[512,2048]{1,0:T(8,128)(2,1)S(1)} %get-tuple-element.8) | data formatting | bytes 4194304
Async XLA Ops:
  0.6 1.2 %copy-start = (bf16[2,128,2048]{2,1,0:T(8,128)(2,1)S(1)}, bf16[2,128,2048]{2,1,0:T(8,128)(2,1)}, u32[]{:S(2)}) copy-start(bf16[2,128,2048]{2,1,0:T(8,128)(2,1)} %param.5) | copy-start | bytes 3145732
  1.9 0.9 %copy-start.1 = (bf16[2,128,512]{2,1,0:T(8,128)(2,1)S(1)}, bf16[2,128,512]{2,1,0:T(8,128)(2,1)}, u32[]{:S(2)}) copy-start(bf16[2,128,512]{2,1,0:T(8,128)(2,1)} %param.6) | copy-start | bytes 786436
  2.8 0.7 copy-start.2
  3.5 0.7 copy-start.3
  4.2 0.7 copy-start.4

commit v5 on v4

--- a/solution.py
+++ b/solution.py
@@ -27,7 +27,7 @@
 
 
 def picker(index, count):
-    rows = lax.broadcasted_iota(jnp.int32, (count, 128), 0)
+    rows = lax.broadcasted_iota(jnp.int32, (count, index.shape[1]), 0)
     return jnp.where(rows == index, 1.0, 0.0).astype(BF)
 
 
@@ -37,6 +37,10 @@
 
 def dot_t(a, b):
     return lax.dot_general(a, b, (((1,), (1,)), ((), ())), preferred_element_type=jnp.float32)
+
+
+def flat(rows):
+    return jnp.concatenate([rows[k : k + 1] for k in range(4)], axis=1)
 
 
 def lanes(parts):
@@ -59,9 +63,9 @@
     return jnp.where(which == 0, rows[0:4], rows[4:8])
 
 
-def kernel(offs, kv, q, keep, dest, attn, mass, owned, recv, spans, keeps, units, goals, own, owns, marks, cz, late, cache, valid, tab, metas, tabl, obuf,
+def kernel(offs, kv, query, keep, dest, attn, mass, owned, recv, q, spans, keeps, units, goals, own, owns, marks, cz, late, cache, valid, tab, metas, tabl, obuf,
            s_sp, s_ke, s_ow, s_ma, s_cz, r_sp, r_ke, r_ow, r_ma, r_cz, s_la, r_la,
-           s_up, r_up, s_dn, r_dn, s_lu, r_lu, s_ld, r_ld, s_ex, r_ex, s_lo, s_un, r_un, s_me, r_me, r_c4, s_c4, s_go, r_go):
+           s_up, r_up, s_dn, r_dn, s_lu, r_lu, s_ld, r_ld, s_ex, r_ex, s_lo, s_un, r_un, s_me, r_me, s_go, r_go, s_q):
     j = lax.axis_index("ctx")
     x = lax.axis_index("kv")
     z = j // 8
@@ -77,9 +81,6 @@
     def pdev(n):
         return (z * 8 + n, x)
 
-    def pair(n, core):
-        return (n * 8 + y * 2 + core, x)
-
     def mdev(n):
         return (z * 8 + n // 4, lax.rem(n, 4))
 
@@ -91,8 +92,7 @@
 
     @pl.loop(1, 8)
     def _(k):
-        for n in range(2):
-            pl.semaphore_signal(barrier, inc=1, device_id=pair(lax.rem(z + k, 8), n), device_id_type=MESH)
+        pl.semaphore_signal(barrier, inc=1, device_id=zdev(lax.rem(z + k, 8)), device_id_type=MESH)
 
     for p in range(2):
         lists = keep[early if p == 0 else 1 - early]
@@ -102,6 +102,7 @@
                 keeps[i, at : at + 1, :] = lists[h : h + 1, k * 128 : (k + 1) * 128]
     for b in range(4):
         spans[i, b * 128 : (b + 1) * 128, :] = kv[early, :, b].reshape(128, 128).T
+    pltpu.make_async_copy(query, q, s_q).start()
     final_pair = j >= 62
 
     @pl.when(final_pair)
@@ -111,7 +112,7 @@
 
     cols = pl.ds(pl.multiple_of(i * 64, 64), 64)
     units[i] = spans[i, cols, :]
-    pl.semaphore_wait(barrier, 45)
+    pl.semaphore_wait(barrier, 38)
 
     def send(src, dst, ss, rs, dev):
         return pltpu.make_async_remote_copy(
@@ -171,8 +172,9 @@
         arrive(units, r_un, lax.rem(i + k, 8))
     head = jnp.where(i < 4, pre[0:4], pre[4:8])
     unit = lanes([units[n] for n in range(8)])
+    picked = dot(unit, picker(flat(head) - 512, 1024)).astype(BF)
     for k in range(4):
-        own[k * 64 : (k + 1) * 64, :] = dot(unit, picker(head[k : k + 1] - 512, 1024)).astype(BF)
+        own[k * 64 : (k + 1) * 64, :] = picked[:, k * 128 : (k + 1) * 128]
     for k in range(1, 8):
         @pl.when(z + k < 8)
         def _():
@@ -198,8 +200,9 @@
         arrive(spans, r_sp, lax.rem(i + k, 8))
     for h in range(2):
         table = lanes([spans[n, h * 256 : (h + 1) * 256, :] for n in range(8)])
+        picked = dot(table, picker(flat(mine[h * 4 : h * 4 + 4]) - 512, 1024)).astype(BF)
         for k in range(4):
-            cache[0, k, h * 256 : (h + 1) * 256, :] = dot(table, picker(mine[h * 4 + k : h * 4 + k + 1] - 512, 1024)).astype(BF)
+            cache[0, k, h * 256 : (h + 1) * 256, :] = picked[:, k * 128 : (k + 1) * 128]
 
     took(goals.at[1 - c], r_go)
     goal0 = half(goals[0], early)
@@ -224,6 +227,102 @@
         copy = send(metas.at[z], metas.at[z], s_me.at[k], r_me.at[z], zdev(lax.rem(z + k, 8)))
         copy.start()
         waits.append(copy)
+
+    own_tokens = lax.broadcasted_iota(jnp.int32, (128, 128), 1) <= lax.broadcasted_iota(jnp.int32, (128, 128), 0)
+
+    def attend(p, h, span_t, low=0, high=8):
+        def chunk(at):
+            return lanes([cache[p, k, at : at + 128, :] for k in range(4)] + [span_t[at : at + 128, :]])
+
+        keys, values = chunk(h * 256), chunk(h * 256 + 128)
+        seen = lanes([jnp.broadcast_to(valid[p, h * 4 + k : h * 4 + k + 1, :], (128, 128)) for k in range(4)]) > 0
+        near = own_tokens
+        prompt = early if p == 0 else 1 - early
+        scale = 1.0 / math.sqrt(HEAD)
+
+        def one(g, total):
+            scores = dot(q[prompt, :, h * 8 + g].reshape(128, 128), keys) * scale
+            old = jnp.where(seen, scores[:, 0:512], -1e30)
+            new = jnp.where(near, scores[:, 512:640], -1e30)
+            peak = jnp.maximum(jnp.max(old, axis=1, keepdims=True), jnp.max(new, axis=1, keepdims=True))
+            expo = lanes([jnp.where(seen, jnp.exp(old - peak), 0.0), jnp.where(near, jnp.exp(new - peak), 0.0)])
+            weights = expo * (1.0 / jnp.sum(expo, axis=1, keepdims=True))
+            mixed = dot_t(weights.astype(BF), values)
+            at = pl.ds(pl.multiple_of((h * 8 + g) * 128, 128), 128)
+            for n in range(2):
+                part = jnp.where(prompt == n, mixed, 0.0)
+                attn[n, :, at] = (part + attn[n, :, at].astype(jnp.float32)).astype(BF)
+            return total + jnp.sum(weights.reshape(16, 8, 640), axis=0)
+
+        total = lax.fori_loop(low, high, one, jnp.zeros((8, 640), jnp.float32))
+        total = jnp.sum(total, axis=0, keepdims=True)
+        for n in range(2):
+            mass[n, h : h + 1, :] += jnp.where(prompt == n, total, 0.0)
+
+    def late_cache():
+        attn[...] = jnp.zeros((2, 128, 2048), BF)
+        mass[...] = jnp.zeros((2, 2, 640), jnp.float32)
+
+        @pl.when(final_pair)
+        def _():
+            took(late.at[1 - c], r_la)
+            for h in range(2):
+                tabl[h] = late[h, pl.ds(pl.multiple_of(c * 256, 256), 256), :]
+            cache[1] = jnp.zeros((4, 512, 128), BF)
+            valid[1] = jnp.zeros((8, 128), jnp.int32)
+
+            @pl.when(c == 1)
+            def _():
+                kept = keeps[first, 8:16, :]
+                valid[1] = jnp.where(kept >= 512, 1, 0)
+                for h in range(2):
+                    for k in range(4):
+                        cache[1, k, h * 256 : (h + 1) * 256, :] = dot(
+                            late[0, h * 256 : (h + 1) * 256, :], picker(kept[h * 4 + k : h * 4 + k + 1] - 512, 128)
+                        ).astype(BF)
+
+    def attend_late(h):
+        @pl.when(final_pair)
+        def _():
+            attend(1, h, late.at[c])
+
+    late_cache()
+    pltpu.make_async_copy(query, q, s_q).wait()
+    attend_late(0)
+
+    above, below = zdev(lax.rem(z + 1, 8)), zdev(lax.rem(z + 7, 8))
+
+    WAYS = (("up", 1), ("down", -1))
+
+    def chunks(way, s):
+        return range(4) if s < 4 else (range(2) if way == "up" else range(2, 4))
+
+    def origin(way, s):
+        return lax.rem(z + 8 - s, 8) if way == "up" else lax.rem(z + s, 8)
+
+    def chunk_copy(way, s, k):
+        o = origin(way, s - 1)
+        ss, rs, to = (s_up, r_up, above) if way == "up" else (s_dn, r_dn, below)
+        return send(tab.at[o, k], tab.at[o, k], ss.at[s * 5 + k], rs.at[s * 5 + k], to)
+
+    def tabl_copy(way):
+        ss, rs, to = (s_lu, r_lu, above) if way == "up" else (s_ld, r_ld, below)
+        return send(tabl, tabl, ss, rs, to)
+
+    def goes(way, s):
+        return s <= (4 if way == "up" else 3)
+
+    def span_start():
+        tab[z, 4] = spans[second, pl.ds(pl.multiple_of(c * 256, 256), 256), :]
+        for way, _ in WAYS:
+            chunk_copy(way, 1, 4).start()
+
+    def span_next(s):
+        for way, _ in WAYS:
+            if goes(way, s):
+                took(tab.at[origin(way, s), 4], (r_up if way == "up" else r_dn).at[s * 5 + 4])
+            if goes(way, s + 1):
+                chunk_copy(way, s + 1, 4).start()
 
     for n in range(7):
         @pl.when(n < z)
@@ -242,44 +341,30 @@
         def _():
             arrive(owns, r_ow, n)
             table = lanes([owns[n, p * 64 : (p + 1) * 64, :] for p in range(4)])
+            picked = dot(table, picker(flat(chead) - n * 512, 512)).astype(BF)
             for k in range(4):
-                part[k * 64 : (k + 1) * 64, :] += dot(table, picker(chead[k : k + 1] - n * 512, 512)).astype(BF)
+                part[k * 64 : (k + 1) * 64, :] += picked[:, k * 128 : (k + 1) * 128]
     for k in range(1, 8):
         copy = send(cz.at[i], cz.at[i], s_cz.at[k], r_cz.at[i], pdev(lax.rem(i + k, 8)))
         copy.start()
         waits.append(copy)
 
-    def span_copies():
-        return [
-            send(spans.at[i, n * 256 : (n + 1) * 256, :], tab.at[z, 4], s_c4.at[k * 2 + n], r_c4.at[z], pair(lax.rem(z + k, 8), n))
-            for k in range(1, 8)
-            for n in range(2)
-        ]
-
-    @pl.when(c == 1)
-    def _():
-        for copy in span_copies():
-            copy.start()
-
+    span_start()
     was = jnp.where(cur >= 0, 1, 0)
     valid[0] = jnp.where(mine >= 512, 1, lookup(was, jnp.minimum(mine, 511)))
 
-    @pl.when(final_pair)
-    def _():
-        took(late.at[1 - c], r_la)
-        for h in range(2):
-            tabl[h] = late[h, pl.ds(pl.multiple_of(c * 256, 256), 256), :]
-
+    span_next(1)
+    attend_late(1)
     for k in range(1, 8):
         arrive(cz, r_cz, lax.rem(i + k, 8))
+    span_next(2)
     for h in range(2):
         table = jnp.concatenate(
             [lanes([cz[n, p * 64 : (p + 1) * 64, :] for p in range(4)]) for n in range(h * 4, h * 4 + 4)], axis=0
         )
+        picked = dot(table, picker(flat(mine[h * 4 : h * 4 + 4]), 512)).astype(BF)
         for k in range(4):
-            cache[0, k, h * 256 : (h + 1) * 256, :] += dot(table, picker(mine[h * 4 + k : h * 4 + k + 1], 512)).astype(BF)
-
-    tab[z, 4] = spans[second, pl.ds(pl.multiple_of(c * 256, 256), 256), :]
+            cache[0, k, h * 256 : (h + 1) * 256, :] += picked[:, k * 128 : (k + 1) * 128]
 
     @pl.when(c == 1)
     def _():
@@ -290,33 +375,12 @@
     def _():
         table = lanes([cache[0, k, 0:256, :] for k in range(4)] + [spans[i, 0:256, :]])
         kept = keeps[i, 0:8, :]
+        picked = dot(table, picker(flat(kept), 640)).astype(BF)
         for k in range(4):
-            tab[z, k] = dot(table, picker(kept[k : k + 1], 640)).astype(BF)
-
-    above, below = zdev(lax.rem(z + 1, 8)), zdev(lax.rem(z + 7, 8))
-
-    WAYS = (("up", 1), ("down", -1))
-
-    def chunks(way, s):
-        return range(4) if s < 4 else (range(2) if way == "up" else range(2, 4))
-
-    def origin(way, s):
-        return lax.rem(z + 8 - s, 8) if way == "up" else lax.rem(z + s, 8)
-
-    def chunk_copy(way, s, k):
-        o = origin(way, s - 1)
-        ss, rs, to = (s_up, r_up, above) if way == "up" else (s_dn, r_dn, below)
-        return send(tab.at[o, k], tab.at[o, k], ss.at[s * 5 + k], rs.at[s * 5 + k], to)
-
-    def tabl_copy(way):
-        ss, rs, to = (s_lu, r_lu, above) if way == "up" else (s_ld, r_ld, below)
-        return send(tabl, tabl, ss, rs, to)
+            tab[z, k] = picked[:, k * 128 : (k + 1) * 128]
 
     def has_late(way, s):
         return (origin(way, s) == 7) & (y == 3)
-
-    def goes(way, s):
-        return s <= (4 if way == "up" else 3)
 
     def lead(s):
         for way, _ in WAYS:
@@ -333,20 +397,24 @@
                     took(tabl, r_lu if way == "up" else r_ld)
         if s < 4:
             lead(s + 1)
+        for task in tasks[:2]:
+            task()
         for k in range(4):
             for way, _ in WAYS:
                 if k in chunks(way, s):
                     took(tab.at[origin(way, s), k], (r_up if way == "up" else r_dn).at[s * 5 + k])
                 if s < 4 and k in chunks(way, s + 1):
                     chunk_copy(way, s + 1, k).start()
-            if k < len(tasks):
-                tasks[k]()
+            if k + 2 < len(tasks):
+                tasks[k + 2]()
 
     def passed(s):
         for way, _ in WAYS:
             for k in chunks(way, s):
                 chunk_copy(way, s, k).wait_send()
             if goes(way, s):
+                chunk_copy(way, s, 4).wait_send()
+
                 @pl.when(has_late(way, s - 1))
                 def _():
                     tabl_copy(way).wait_send()
@@ -384,76 +452,23 @@
 
         keep_local(o).start()
 
-    own_tokens = lax.broadcasted_iota(jnp.int32, (128, 128), 1) <= lax.broadcasted_iota(jnp.int32, (128, 128), 0)
-
-    def attend(p, h, span_t):
-        def chunk(at):
-            return lanes([cache[p, k, at : at + 128, :] for k in range(4)] + [span_t[at : at + 128, :]])
-
-        keys, values = chunk(h * 256), chunk(h * 256 + 128)
-        seen = lanes([jnp.broadcast_to(valid[p, h * 4 + k : h * 4 + k + 1, :], (128, 128)) for k in range(4)]) > 0
-        near = own_tokens
-        prompt = early if p == 0 else 1 - early
-        scale = 1.0 / math.sqrt(HEAD)
-
-        def one(g, total):
-            scores = dot(q[prompt, :, h * 8 + g].reshape(128, 128), keys) * scale
-            old = jnp.where(seen, scores[:, 0:512], -1e30)
-            new = jnp.where(near, scores[:, 512:640], -1e30)
-            peak = jnp.maximum(jnp.max(old, axis=1, keepdims=True), jnp.max(new, axis=1, keepdims=True))
-            expo = lanes([jnp.where(seen, jnp.exp(old - peak), 0.0), jnp.where(near, jnp.exp(new - peak), 0.0)])
-            weights = expo * (1.0 / jnp.sum(expo, axis=1, keepdims=True))
-            mixed = dot_t(weights.astype(BF), values)
-            at = pl.ds(pl.multiple_of((h * 8 + g) * 128, 128), 128)
-            for n in range(2):
-                part = jnp.where(prompt == n, mixed, 0.0)
-                if p == 1:
-                    part = part + attn[n, :, at].astype(jnp.float32)
-                attn[n, :, at] = part.astype(BF)
-            return total + jnp.sum(weights.reshape(16, 8, 640), axis=0)
-
-        total = lax.fori_loop(0, 8, one, jnp.zeros((8, 640), jnp.float32))
-        total = jnp.sum(total, axis=0, keepdims=True)
-        for n in range(2):
-            part = jnp.where(prompt == n, total, 0.0)
-            mass[n, h : h + 1, :] = part + mass[n, h : h + 1, :] if p == 1 else part
-
-    def attend_late():
-        @pl.when(final_pair)
-        def _():
-            cache[1] = jnp.zeros((4, 512, 128), BF)
-            valid[1] = jnp.zeros((8, 128), jnp.int32)
-
-            @pl.when(c == 1)
-            def _():
-                kept = keeps[first, 8:16, :]
-                valid[1] = jnp.where(kept >= 512, 1, 0)
-                for h in range(2):
-                    for k in range(4):
-                        cache[1, k, h * 256 : (h + 1) * 256, :] = dot(
-                            late[0, h * 256 : (h + 1) * 256, :], picker(kept[h * 4 + k : h * 4 + k + 1] - 512, 128)
-                        ).astype(BF)
-
-            for h in range(2):
-                attend(1, h, late.at[c])
-
     lead(1)
     for k in range(4):
         for way, _ in WAYS:
             chunk_copy(way, 1, k).start()
+    span_next(3)
 
     def hand_in(o):
         arrive(metas, r_me, o)
-        took(tab.at[o, 4], r_c4.at[o])
         hand_out(o)
 
     def hand(way, s):
         return lambda: hand_in(origin(way, s))
 
     hand_out(z)
-    receive(1, [lambda: attend(0, 0, spans.at[i])])
-    receive(2, [hand("up", 1), hand("down", 1), lambda: attend(0, 1, spans.at[i])])
-    receive(3, [hand("up", 2), hand("down", 2), attend_late])
+    receive(1, [lambda: span_next(4), lambda: attend(0, 0, spans.at[i], 0, 3), lambda: attend(0, 0, spans.at[i], 3, 6)])
+    receive(2, [hand("up", 1), hand("down", 1), lambda: attend(0, 0, spans.at[i], 6, 8), lambda: attend(0, 1, spans.at[i], 0, 2)])
+    receive(3, [hand("up", 2), hand("down", 2), lambda: attend(0, 1, spans.at[i], 2, 5), lambda: attend(0, 1, spans.at[i], 5, 8)])
     receive(4, [hand("up", 3), hand("down", 3)])
     hand_in(origin("up", 4))
 
@@ -464,11 +479,6 @@
         def _():
             marks_copy(k).wait_send()
             own_copy(k).wait_send()
-
-    @pl.when(c == 1)
-    def _():
-        for copy in span_copies():
-            copy.wait_send()
 
     @pl.when(final_pair)
     def _():
@@ -497,10 +507,11 @@
             jax.ShapeDtypeStruct((2, 2, 640), jnp.float32),
             jax.ShapeDtypeStruct((512, 2048), BF),
         ),
-        in_specs=[pl.BlockSpec(memory_space=pltpu.SMEM)] + [vmem] * 4,
+        in_specs=[pl.BlockSpec(memory_space=pltpu.SMEM), vmem, pl.BlockSpec(memory_space=pl.ANY), vmem, vmem],
         out_specs=(vmem,) * 3,
         scratch_shapes=[
             V((16, 512, 128), BF),
+            V((2, 16, 16, 8, 128), BF),
             V((8, 512, 128), BF),
             V((8, 16, 128), jnp.int32),
             V((8, 64, 128), BF),
@@ -521,9 +532,8 @@
         + [D] * 2
         + [D((25,))] * 4
         + [D] * 4
-        + [D((8,))] * 8
-        + [D((16,))]
-        + [D] * 2,
+        + [D((8,))] * 7
+        + [D] * 3,
         compiler_params=pltpu.CompilerParams(collective_id=0, has_side_effects=True, vmem_limit_bytes=40 << 20),
     )(offsets, kv, q, keep, dest)
 

time: 94.3 us -> 91.5 us (0.970)
  the two profiles are of different devices: /device:TPU:225 before, /device:TPU:1 now
where the time goes in v5:
time: 91.5 us; the launch traced here: 91.2 us
  Pallas kernels  83.5 us (91%)
  local copies, waits for them, and re-layouts  7.09 us (8%)
    pallas_call x1, Pallas kernels, whole(): pl.pallas_call(kernel, out_shape=(jax.ShapeDtypeStruct((2, 128, 2048), BF...  83.5 us
    unnamed x13, local copies, waits for them, and re-layouts  7.09 us

profile of v5, /device:TPU:1, one launch (start us, length us, event | category | flops | bytes accessed | tf_op | source)
XLA Modules:
  0.0 91.2 jit_solution(1261759243468291533)
XLA Ops:
  0.6 0.0 copy-start
  0.6 1.2 %copy-done = bf16[2,128,2048]{2,1,0:T(8,128)(2,1)S(1)} copy-done((bf16[2,128,2048]{2,1,0:T(8,128)(2,1)S(1)}, bf16[2,128,2048]{2,1,0:T(8,128)(2,1)}, u32[]{:S(2)}) %copy-start) | copy-done | bytes 1048600
  1.9 0.0 copy-start.1
  1.9 0.9 %copy-done.1 = bf16[2,128,512]{2,1,0:T(8,128)(2,1)S(1)} copy-done((bf16[2,128,512]{2,1,0:T(8,128)(2,1)S(1)}, bf16[2,128,512]{2,1,0:T(8,128)(2,1)}, u32[]{:S(2)}) %copy-start.1) | copy-done | bytes 262168
  2.8 0.0 copy-start.2
  2.8 0.7 copy-done.2
  3.5 0.0 copy-start.3
  3.5 0.7 copy-done.3
  4.2 0.0 copy-start.4
  4.2 0.7 copy-done.4
  4.8 83.5 %shard_map.76 = (bf16[2,128,2048]{2,1,0:T(8,128)(2,1)S(1)}, f32[2,2,640]{2,1,0:T(2,128)S(1)}, bf16[512,2048]{1,0:T(8,128)(2,1)S(1)}) custom-call(s32[2]{0:T(128)S(1)} %copy-done.4, bf16[2,16,4,8,128]{4,3,2,1,0:T(8,128)(2,1)S(1)} %bitcast.9, bf16[2,16,16,8,128]{4,3,2,1,0:T(8,128)(2,1)S(1)} %bitcast.8, s32[2,2,512]{2,1,0:T(2,128)S(1)} %bitcast.10, ...), custom_call_target="tpu_custom_call" | custom-call | tf_op jit(solution)/shard_map/pallas_call | solution.py:503
  88.4 1.0 %copy.11 = bf16[2,128,2048]{2,1,0:T(8,128)(2,1)} copy(bf16[2,128,2048]{2,1,0:T(8,128)(2,1)S(1)} %get-tuple-element.6) | data formatting | bytes 2097152
  89.3 0.6 copy.12
  89.9 1.3 %copy.13 = bf16[512,2048]{1,0:T(8,128)(2,1)} copy(bf16[512,2048]{1,0:T(8,128)(2,1)S(1)} %get-tuple-element.8) | data formatting | bytes 4194304
Async XLA Ops:
  0.6 1.2 %copy-start = (bf16[2,128,2048]{2,1,0:T(8,128)(2,1)S(1)}, bf16[2,128,2048]{2,1,0:T(8,128)(2,1)}, u32[]{:S(2)}) copy-start(bf16[2,128,2048]{2,1,0:T(8,128)(2,1)} %param.5) | copy-start | bytes 3145732
  1.9 0.9 %copy-start.1 = (bf16[2,128,512]{2,1,0:T(8,128)(2,1)S(1)}, bf16[2,128,512]{2,1,0:T(8,128)(2,1)}, u32[]{:S(2)}) copy-start(bf16[2,128,512]{2,1,0:T(8,128)(2,1)} %param.6) | copy-start | bytes 786436
  2.8 0.7 copy-start.2
  3.5 0.7 copy-start.3
  4.2 0.7 copy-start.4

commit v6 on v5

--- a/solution.py
+++ b/solution.py
@@ -419,9 +419,9 @@
                 def _():
                     tabl_copy(way).wait_send()
 
-    def exchange(o, n):
+    def exchange(o, n, m):
         dst = recv.at[pl.ds(x * 4 + c * 2, 2), pl.ds(pl.multiple_of((o * 4 + y) * 16, 16), 16), :]
-        return send(obuf.at[o, :, pl.ds(pl.multiple_of(n * 16, 16), 16), :], dst, s_ex.at[o], r_ex.at[o], mdev(n))
+        return send(obuf.at[o, :, pl.ds(pl.multiple_of((n * 4 + m) * 16, 16), 16), :], dst, s_ex.at[o], r_ex.at[o], (z * 8 + n, m))
 
     def keep_local(o):
         dst = recv.at[pl.ds(x * 4 + c * 2, 2), pl.ds(pl.multiple_of((o * 4 + y) * 16, 16), 16), :]
@@ -446,9 +446,14 @@
             obuf[o, 0] += rows[:, 0:128]
             obuf[o, 1] += rows[:, 128:256]
 
-        @pl.loop(1, 32)
+        for d in range(1, 4):
+            exchange(o, i, lax.rem(x + d, 4)).start()
+
+        @pl.loop(1, 8)
         def _(k):
-            exchange(o, lax.rem(me + k, 32)).start()
+            n = lax.rem(i + k, 8)
+            for d in range(4):
+                exchange(o, n, lax.rem(x + d, 4)).start()
 
         keep_local(o).start()
 

time: 91.5 us -> 91.8 us (level)
  no operation moved by 1% of the time
where the time goes in v6:
time: 91.8 us; the launch traced here: 91.6 us
  Pallas kernels  83.8 us (91%)
  local copies, waits for them, and re-layouts  7.09 us (8%)
    pallas_call x1, Pallas kernels, whole(): pl.pallas_call(kernel, out_shape=(jax.ShapeDtypeStruct((2, 128, 2048), BF...  83.8 us
    unnamed x13, local copies, waits for them, and re-layouts  7.09 us

profile of v6, /device:TPU:1, one launch (start us, length us, event | category | flops | bytes accessed | tf_op | source)
XLA Modules:
  0.0 91.6 jit_solution(15872174277644881823)
XLA Ops:
  0.6 0.0 copy-start
  0.6 1.2 %copy-done = bf16[2,128,2048]{2,1,0:T(8,128)(2,1)S(1)} copy-done((bf16[2,128,2048]{2,1,0:T(8,128)(2,1)S(1)}, bf16[2,128,2048]{2,1,0:T(8,128)(2,1)}, u32[]{:S(2)}) %copy-start) | copy-done | bytes 1048600
  1.9 0.0 copy-start.1
  1.9 0.9 %copy-done.1 = bf16[2,128,512]{2,1,0:T(8,128)(2,1)S(1)} copy-done((bf16[2,128,512]{2,1,0:T(8,128)(2,1)S(1)}, bf16[2,128,512]{2,1,0:T(8,128)(2,1)}, u32[]{:S(2)}) %copy-start.1) | copy-done | bytes 262168
  2.8 0.0 copy-start.2
  2.8 0.7 copy-done.2
  3.5 0.0 copy-start.3
  3.5 0.7 copy-done.3
  4.2 0.0 copy-start.4
  4.2 0.7 copy-done.4
  4.8 83.8 %shard_map.76 = (bf16[2,128,2048]{2,1,0:T(8,128)(2,1)S(1)}, f32[2,2,640]{2,1,0:T(2,128)S(1)}, bf16[512,2048]{1,0:T(8,128)(2,1)S(1)}) custom-call(s32[2]{0:T(128)S(1)} %copy-done.4, bf16[2,16,4,8,128]{4,3,2,1,0:T(8,128)(2,1)S(1)} %bitcast.9, bf16[2,16,16,8,128]{4,3,2,1,0:T(8,128)(2,1)S(1)} %bitcast.8, s32[2,2,512]{2,1,0:T(2,128)S(1)} %bitcast.10, ...), custom_call_target="tpu_custom_call" | custom-call | tf_op jit(solution)/shard_map/pallas_call | solution.py:508
  88.7 1.0 %copy.11 = bf16[2,128,2048]{2,1,0:T(8,128)(2,1)} copy(bf16[2,128,2048]{2,1,0:T(8,128)(2,1)S(1)} %get-tuple-element.6) | data formatting | bytes 2097152
  89.7 0.6 copy.12
  90.3 1.3 %copy.13 = bf16[512,2048]{1,0:T(8,128)(2,1)} copy(bf16[512,2048]{1,0:T(8,128)(2,1)S(1)} %get-tuple-element.8) | data formatting | bytes 4194304
Async XLA Ops:
  0.6 1.2 %copy-start = (bf16[2,128,2048]{2,1,0:T(8,128)(2,1)S(1)}, bf16[2,128,2048]{2,1,0:T(8,128)(2,1)}, u32[]{:S(2)}) copy-start(bf16[2,128,2048]{2,1,0:T(8,128)(2,1)} %param.5) | copy-start | bytes 3145732
  1.9 0.9 %copy-start.1 = (bf16[2,128,512]{2,1,0:T(8,128)(2,1)S(1)}, bf16[2,128,512]{2,1,0:T(8,128)(2,1)}, u32[]{:S(2)}) copy-start(bf16[2,128,512]{2,1,0:T(8,128)(2,1)} %param.6) | copy-start | bytes 786436
  2.8 0.7 copy-start.2
  3.5 0.7 copy-start.3
  4.2 0.7 copy-start.4
